TPU v7x, 32 devices: a whole 2x2x4 slice. The times are simulated.
32 devices in a mesh: dp: 8 (over y, x, core), seq: 4 (over z).
Axes of the slice: x: 2, y: 2, z: 4, core: 2. Of those that a mesh axis runs over, the one named last changes fastest.
Arguments:
- inputs: bfloat16 [16, 2048, 512], P('dp', 'seq'), may hold values from -6 to 6
- segment_ids: int32 [16, 2048], P('dp'), may hold values from 0 to 6, as said below
- cotangent: bfloat16 [16, 2048, 512], P('dp', 'seq'), may hold values from -6 to 6
- norm_attn: float32 [512], replicated, may hold values from 0.1 to 1.9
- norm_mlp: float32 [512], replicated, may hold values from 0.1 to 1.9
- w_query: bfloat16 [512, 512], replicated, may hold values from -0.25 to 0.25
- w_key: bfloat16 [512, 512], replicated, may hold values from -0.25 to 0.25
- w_value: bfloat16 [512, 512], replicated, may hold values from -0.25 to 0.25
- w_out: bfloat16 [512, 512], replicated, may hold values from -1.5 to 1.5
- w_gate: bfloat16 [512, 1376], replicated, may hold values from -0.25 to 0.25
- w_up: bfloat16 [512, 1376], replicated, may hold values from -0.25 to 0.25
- w_down: bfloat16 [1376, 512], replicated, may hold values from -0.15625 to 0.15625
Outputs:
- output: bfloat16 [16, 2048, 512], P('dp', 'seq')
- grad_input: float32 [16, 2048, 512], P('dp', 'seq')
- grad_norm_attn: float32 [512], replicated
- grad_norm_mlp: float32 [512], replicated
- grad_query: float32 [512, 512], replicated
- grad_key: float32 [512, 512], replicated
- grad_value: float32 [512, 512], replicated
- grad_out: float32 [512, 512], replicated
- grad_gate: float32 [512, 1376], replicated
- grad_up: float32 [512, 1376], replicated
- grad_down: float32 [1376, 512], replicated
Inputs may be any that keep to these rules, and one draw needn't show every extreme that they name: `segment_ids`: segment ids never fall along a sequence; in every sequence the documents before the middle one end within its first 128 tokens, and the ones after it begin within its last 128 tokens; the first token has id 0 and the last id 6.
All inputs are finite; a program needn't handle non-finite values.
Results may differ from a plain program's by a relative error of at most 0.014.
Values may be sent and summed in bfloat16 or wider, within the bound.
A program may use at most 128 MiB of HBM per device.

v0:
```python
import jax
import jax.numpy as jnp
from jax import lax
from jax.sharding import PartitionSpec as P

MICRO = 2
DOCS = 7
HD = 64


epsilon = 1e-05
theta_base = 10000.0
masked_value = -1e30


def rope_tables(segment_ids):
    documents = jnp.arange(DOCS, dtype=jnp.int32)
    member = (segment_ids[:, :, None] == documents[None, None, :]).astype(jnp.int32)
    doc_sizes = jnp.sum(member, axis=1)
    earlier = (documents[None, None, :] < segment_ids[:, :, None]).astype(jnp.int32)
    first_token = jnp.sum(earlier * doc_sizes[:, None, :], axis=-1)
    place = jnp.arange(segment_ids.shape[1], dtype=jnp.int32)[None, :] - first_token
    half_dim = HD // 2
    frequency = theta_base ** (-2.0 * jnp.arange(half_dim, dtype=jnp.float32) / HD)
    angle = place.astype(jnp.float32)[:, :, None] * frequency[None, None, :]
    angle = jnp.concatenate([angle, angle], axis=-1)
    return (jnp.cos(angle), jnp.sin(angle))


def rotate(values, cosine, sine_table):
    half_dim = values.shape[-1] // 2
    turned = jnp.concatenate([-values[..., half_dim:], values[..., :half_dim]], axis=-1)
    return values * cosine[:, :, None, :] + turned * sine_table[:, :, None, :]


def unrotate(grads, cosine, sine_table):
    half_dim = grads.shape[-1] // 2
    scaled = grads * sine_table[:, :, None, :]
    turned = jnp.concatenate([scaled[..., half_dim:], -scaled[..., :half_dim]], axis=-1)
    return grads * cosine[:, :, None, :] + turned


def rms_parts(values):
    inverse = lax.rsqrt(jnp.mean(values * values, axis=-1, keepdims=True) + epsilon)
    return (values * inverse, inverse)


def rms_back(d_normed, plain, inverse, gain):
    scaled = d_normed * gain
    grad_gain = jnp.sum(d_normed * plain, axis=(0, 1))
    d_values = inverse * (scaled - plain * jnp.mean(scaled * plain, axis=-1, keepdims=True))
    return (d_values, grad_gain)


def block_mask(seg_row, block_start, block_rows):
    query_seg = lax.dynamic_slice_in_dim(seg_row, block_start, block_rows, 0)
    query_place = block_start + jnp.arange(block_rows, dtype=jnp.int32)
    key_place = jnp.arange(seg_row.shape[0], dtype=jnp.int32)
    return (key_place[None, :] <= query_place[:, None]) & (query_seg[:, None] == seg_row[None, :])


def masked_scores(block_query, key_rows, seg_row, block_start):
    block_rows = block_query.shape[0]
    scores = jnp.einsum(
        "qhd,khd->hqk", block_query, key_rows, preferred_element_type=jnp.float32
    ) * HD ** (-0.5)
    allowed = block_mask(seg_row, block_start, block_rows)
    return jnp.where(allowed[None], scores, masked_value)


def attend_forward(query, keys, values, seg_group):
    seq_total, length, heads_here, head_dim = query.shape
    block_rows = min(512, length)
    blocks = length // block_rows

    def one_block(block_index):
        owner_index = block_index // blocks
        block_start = block_index % blocks * block_rows
        seq_query = lax.dynamic_index_in_dim(query, owner_index, 0, keepdims=False)
        key_rows = lax.dynamic_index_in_dim(keys, owner_index, 0, keepdims=False)
        value_rows = lax.dynamic_index_in_dim(values, owner_index, 0, keepdims=False)
        seg_row = lax.dynamic_index_in_dim(seg_group, owner_index, 0, keepdims=False)
        block_query = lax.dynamic_slice_in_dim(seq_query, block_start, block_rows, 0)
        masked = masked_scores(block_query, key_rows, seg_row, block_start)
        row_top = jnp.max(masked, axis=-1, keepdims=True)
        expanded = jnp.exp(masked - row_top)
        row_total = jnp.sum(expanded, axis=-1, keepdims=True)
        weights_low = (expanded / row_total).astype(jnp.bfloat16)
        attended = jnp.einsum(
            "hqk,khd->qhd", weights_low, value_rows, preferred_element_type=jnp.float32
        )
        log_total = row_top[:, :, 0] + jnp.log(row_total[:, :, 0])
        return (attended.reshape(block_rows, heads_here * head_dim), log_total)

    attended, log_total = lax.map(one_block, jnp.arange(seq_total * blocks, dtype=jnp.int32))
    attended = attended.reshape(seq_total, length, heads_here * head_dim)
    log_total = log_total.reshape(seq_total, blocks, heads_here, block_rows)
    return (attended, log_total)


def attend_backward(query, keys, values, d_out, log_total, seg_group):
    seq_total, length, heads_here, head_dim = query.shape
    block_rows = min(512, length)
    blocks = length // block_rows
    score_scale = HD ** (-0.5)

    def one_sequence(owner_index):
        seq_query = lax.dynamic_index_in_dim(query, owner_index, 0, keepdims=False)
        key_rows = lax.dynamic_index_in_dim(keys, owner_index, 0, keepdims=False)
        value_rows = lax.dynamic_index_in_dim(values, owner_index, 0, keepdims=False)
        seq_grad = lax.dynamic_index_in_dim(d_out, owner_index, 0, keepdims=False)
        seq_log = lax.dynamic_index_in_dim(log_total, owner_index, 0, keepdims=False)
        seg_row = lax.dynamic_index_in_dim(seg_group, owner_index, 0, keepdims=False)

        def step_block(partial_value, block_index):
            d_keys, d_values = partial_value
            block_start = block_index * block_rows
            block_query = lax.dynamic_slice_in_dim(seq_query, block_start, block_rows, 0)
            block_grad = lax.dynamic_slice_in_dim(seq_grad, block_start, block_rows, 0)
            block_log = lax.dynamic_index_in_dim(seq_log, block_index, 0, keepdims=False)
            masked = masked_scores(block_query, key_rows, seg_row, block_start)
            probs = jnp.exp(masked - block_log[:, :, None])
            weights_low = probs.astype(jnp.bfloat16)
            d_values = d_values + jnp.einsum(
                "hqk,qhd->khd", weights_low, block_grad, preferred_element_type=jnp.float32
            )
            d_probs = jnp.einsum(
                "qhd,khd->hqk", block_grad, value_rows, preferred_element_type=jnp.float32
            )
            row_delta = jnp.sum(probs * d_probs, axis=-1, keepdims=True)
            d_scores = (probs * (d_probs - row_delta)).astype(jnp.bfloat16)
            d_query = (
                jnp.einsum("hqk,khd->qhd", d_scores, key_rows, preferred_element_type=jnp.float32)
                * score_scale
            )
            d_keys = d_keys + jnp.einsum(
                "hqk,qhd->khd", d_scores, block_query, preferred_element_type=jnp.float32
            )
            return ((d_keys, d_values), d_query)

        zeros_kv = jnp.zeros((length, heads_here, head_dim), jnp.float32)
        (d_keys, d_values), d_query = lax.scan(
            step_block, (zeros_kv, zeros_kv), jnp.arange(blocks, dtype=jnp.int32)
        )
        return (d_query.reshape(length, heads_here, head_dim), d_keys * score_scale, d_values)

    return lax.map(one_sequence, jnp.arange(seq_total, dtype=jnp.int32))


def flat_dot(left, right):
    return jnp.dot(left, right, preferred_element_type=jnp.float32)


def token_sum(left, right):
    return jnp.einsum("ti,tj->ij", left, right, preferred_element_type=jnp.float32)


def layer_step(rows_in, seg_group, grad_rows, cosine, sine_table, gain_attn, gain_mlp, weights):
    w_query, w_key, w_value, w_out, w_gate, w_up, w_down = weights
    seq_count, row_count, model_width = rows_in.shape
    tokens = seq_count * row_count
    row_shape = (seq_count, row_count, model_width)
    row_heads = (seq_count, row_count, model_width // HD, HD)
    start_x = rows_in.astype(jnp.float32)
    plain_attn, inverse_attn = rms_parts(start_x)
    normed_attn = (plain_attn * gain_attn).astype(jnp.bfloat16).reshape(tokens, model_width)
    query_lin = flat_dot(normed_attn, w_query).reshape(row_heads)
    key_lin = flat_dot(normed_attn, w_key).reshape(row_heads)
    value_lin = flat_dot(normed_attn, w_value)
    query_low = rotate(query_lin, cosine, sine_table).reshape(row_shape).astype(jnp.bfloat16)
    key_low = rotate(key_lin, cosine, sine_table).reshape(row_shape).astype(jnp.bfloat16)
    value_low = value_lin.reshape(row_shape).astype(jnp.bfloat16)
    query_heads, key_heads, value_heads = (
        lax.all_to_all(query_low, "seq", split_axis=2, concat_axis=1, tiled=True),
        lax.all_to_all(key_low, "seq", split_axis=2, concat_axis=1, tiled=True),
        lax.all_to_all(value_low, "seq", split_axis=2, concat_axis=1, tiled=True),
    )
    length = query_heads.shape[1]
    head_shape = (seq_count, length, query_heads.shape[2] // HD, HD)
    query_split = query_heads.reshape(head_shape)
    key_split = key_heads.reshape(head_shape)
    value_split = value_heads.reshape(head_shape)
    attended, log_total = attend_forward(query_split, key_split, value_split, seg_group)
    mixed = lax.all_to_all(
        attended.astype(jnp.bfloat16), "seq", split_axis=1, concat_axis=2, tiled=True
    )
    flat_mixed = mixed.reshape(tokens, model_width)
    middle = start_x + flat_dot(flat_mixed, w_out).reshape(row_shape)
    plain_mlp, inverse_mlp = rms_parts(middle)
    normed_mlp = (plain_mlp * gain_mlp).astype(jnp.bfloat16).reshape(tokens, model_width)
    gate_value = flat_dot(normed_mlp, w_gate)
    up_value = flat_dot(normed_mlp, w_up)
    sigmoid_gate = jax.nn.sigmoid(gate_value)
    activated = gate_value * sigmoid_gate
    hidden = (activated * up_value).astype(jnp.bfloat16)
    result = (middle + flat_dot(hidden, w_down).reshape(row_shape)).astype(jnp.bfloat16)
    grad_flat = grad_rows.reshape(tokens, model_width)
    grad_down = token_sum(hidden, grad_flat)
    d_hidden = flat_dot(grad_flat, w_down.T)
    d_gate = (
        d_hidden * up_value * sigmoid_gate * (1.0 + gate_value * (1.0 - sigmoid_gate))
    ).astype(jnp.bfloat16)
    d_up = (d_hidden * activated).astype(jnp.bfloat16)
    grad_gate = token_sum(normed_mlp, d_gate)
    grad_up = token_sum(normed_mlp, d_up)
    d_normed_mlp = (flat_dot(d_gate, w_gate.T) + flat_dot(d_up, w_up.T)).reshape(row_shape)
    d_middle_part, grad_gain_mlp = rms_back(d_normed_mlp, plain_mlp, inverse_mlp, gain_mlp)
    d_middle = grad_rows.astype(jnp.float32) + d_middle_part
    d_attn = d_middle.astype(jnp.bfloat16).reshape(tokens, model_width)
    grad_out = token_sum(flat_mixed, d_attn)
    d_mixed = flat_dot(d_attn, w_out.T).astype(jnp.bfloat16).reshape(row_shape)
    d_heads = lax.all_to_all(d_mixed, "seq", split_axis=2, concat_axis=1, tiled=True)
    d_query, d_keys, d_values = attend_backward(
        query_split, key_split, value_split, d_heads.reshape(head_shape), log_total, seg_group
    )
    flat_heads = (seq_count, length, head_shape[2] * HD)
    back_query, back_keys, back_values = (
        lax.all_to_all(
            d_query.reshape(flat_heads).astype(jnp.bfloat16),
            "seq",
            split_axis=1,
            concat_axis=2,
            tiled=True,
        ),
        lax.all_to_all(
            d_keys.reshape(flat_heads).astype(jnp.bfloat16),
            "seq",
            split_axis=1,
            concat_axis=2,
            tiled=True,
        ),
        lax.all_to_all(
            d_values.reshape(flat_heads).astype(jnp.bfloat16),
            "seq",
            split_axis=1,
            concat_axis=2,
            tiled=True,
        ),
    )
    d_query_lin = (
        unrotate(back_query.astype(jnp.float32).reshape(row_heads), cosine, sine_table)
        .astype(jnp.bfloat16)
        .reshape(tokens, model_width)
    )
    d_key_lin = (
        unrotate(back_keys.astype(jnp.float32).reshape(row_heads), cosine, sine_table)
        .astype(jnp.bfloat16)
        .reshape(tokens, model_width)
    )
    d_value_flat = back_values.reshape(tokens, model_width)
    grad_query = token_sum(normed_attn, d_query_lin)
    grad_key = token_sum(normed_attn, d_key_lin)
    grad_value = token_sum(normed_attn, d_value_flat)
    d_normed_attn = (
        flat_dot(d_query_lin, w_query.T)
        + flat_dot(d_key_lin, w_key.T)
        + flat_dot(d_value_flat, w_value.T)
    )
    d_start_part, grad_gain_attn = rms_back(
        d_normed_attn.reshape(row_shape), plain_attn, inverse_attn, gain_attn
    )
    grad_input = d_middle + d_start_part
    return (
        result,
        grad_input,
        (
            grad_gain_attn,
            grad_gain_mlp,
            grad_query,
            grad_key,
            grad_value,
            grad_out,
            grad_gate,
            grad_up,
            grad_down,
        ),
    )


def on_device(
    inputs,
    segment_ids,
    cotangent,
    norm_attn,
    norm_mlp,
    w_query,
    w_key,
    w_value,
    w_out,
    w_gate,
    w_up,
    w_down,
):
    group_seqs, row_count, model_width = inputs.shape
    per_micro = group_seqs // MICRO
    cosine_all, sine_all = rope_tables(segment_ids)
    offset = lax.axis_index("seq") * row_count
    cosine_rows = lax.dynamic_slice_in_dim(cosine_all, offset, row_count, 1)
    sine_rows = lax.dynamic_slice_in_dim(sine_all, offset, row_count, 1)
    weights = (w_query, w_key, w_value, w_out, w_gate, w_up, w_down)
    totals = None
    outputs = []
    input_grads = []
    for micro_index in range(MICRO):
        first_seq = micro_index * per_micro
        last_seq = first_seq + per_micro
        result, grad_input, grads = layer_step(
            inputs[first_seq:last_seq],
            segment_ids[first_seq:last_seq],
            cotangent[first_seq:last_seq],
            cosine_rows[first_seq:last_seq],
            sine_rows[first_seq:last_seq],
            norm_attn,
            norm_mlp,
            weights,
        )
        outputs.append(result)
        input_grads.append(grad_input)
        if totals is None:
            totals = tuple(grads)
        else:
            totals = tuple((total + grad for total, grad in zip(totals, grads)))
    sum_ga, sum_gm, sum_wq, sum_wk, sum_wv, sum_wo, sum_wg, sum_wu, sum_wd = totals
    totals = lax.psum(
        (sum_ga, sum_gm, sum_wq, sum_wk, sum_wv, sum_wo, sum_wg, sum_wu, sum_wd), ("dp", "seq")
    )
    output = jnp.concatenate(outputs, axis=0)
    grad_input_all = jnp.concatenate(input_grads, axis=0)
    return (
        output,
        grad_input_all,
        totals[0],
        totals[1],
        totals[2],
        totals[3],
        totals[4],
        totals[5],
        totals[6],
        totals[7],
        totals[8],
    )


def solution(mesh):
    placed = (
        P("dp", "seq", None),
        P("dp", None),
        P("dp", "seq", None),
        P(),
        P(),
        P(),
        P(),
        P(),
        P(),
        P(),
        P(),
        P(),
    )
    return jax.shard_map(
        on_device,
        mesh=mesh,
        in_specs=placed,
        out_specs=(
            P("dp", "seq", None),
            P("dp", "seq", None),
            P(),
            P(),
            P(),
            P(),
            P(),
            P(),
            P(),
            P(),
            P(),
        ),
        check_vma=False,
    )
```

profile of v0, /device:TPU:0, one launch (start us, length us, event | category | flops | bytes accessed | tf_op | source)
XLA Modules:
  0.0 1129.7 jit_solution(5085439493897093349)
XLA Ops:
  27.7 6.5 all-to-all-start.1
  42.9 5.9 all-to-all-done.1
  139.4 47.3 %while.80 = (s32[]{:T(128)}, bf16[4,512,128]{2,1,0:T(8,128)(2,1)S(1)}, f32[4,2,512]{2,1,0:T(2,128)S(1)}, s32[4]{0:T(128)S(1)}, s32[1,2048]{1,0:T(1,128)S(1)}, /*...) while((s32[]{:T(128)}, ...), condition=%wide.region_6.7_spmd, body=%wide.region_3.6_spmd.sunk | while | flops 565181952 | bytes 33343836 | solution.py:95
  189.2 12.4 %reduce.15 = bf16[2048,128]{1,0:T(8,128)(2,1)} reduce(bf16[2048,1,128]{2,1,0:T(2,128)(2,1)S(1)} %bitcast.621, bf16[]{:T(256)} %broadcast.544), dimensions={1}, to_apply=%bitcast.499.reduce_sub_computation | reduce | bytes 1048578
  219.6 48.1 %while.81 = (s32[]{:T(128)}, bf16[4,512,128]{2,1,0:T(8,128)(2,1)S(1)}, f32[4,2,512]{2,1,0:T(2,128)S(1)}, s32[4]{0:T(128)S(1)}, s32[1,2048]{1,0:T(1,128)S(1)}, /*...) while((s32[]{:T(128)}, ...), condition=%wide.region_12.13_spmd, body=%wide.region_9.12_spmd.sunk | while | flops 565181952 | bytes 31246656 | solution.py:95
  267.7 8.1 copy.519
  275.9 11.7 %reduce.11 = bf16[2048,128]{1,0:T(8,128)(2,1)S(1)} reduce(bf16[2048,1,128]{2,1,0:T(2,128)(2,1)S(1)} %bitcast.622, bf16[]{:T(256)} %broadcast.544), dimensions={1}, to_apply=%bitcast.496.reduce_sub_computation | reduce | bytes 1048578
  377.1 137.3 %while.83 = (s32[]{:T(128)}, f32[2048,2,64]{0,2,1:T(8,128)}, f32[2048,2,64]{0,2,1:T(8,128)}, bf16[4,512,2,64]{1,3,2,0:T(8,128)(2,1)}, s32[4]{0:T(128)S(1)}, /*in...) while((s32[]{:T(128)}, f32[2048,2,64]{0,2,1:T(8,128)}, ...), condition=%wide.region_22.23_spmd.clone, body=%wide.region_20.22_spmd.clone.sunk | while | flops 1377893888 | bytes 132430696 | solution.py:142
  379.5 5.7 fusion.342
  387.1 6.8 multiply_reduce_fusion.7
  413.3 5.7 fusion.342
  420.9 6.8 multiply_reduce_fusion.7
  447.8 5.7 fusion.342
  455.4 6.8 multiply_reduce_fusion.7
  482.3 5.7 fusion.342
  489.9 6.8 multiply_reduce_fusion.7
  518.9 12.4 %reduce.23 = bf16[2048,128]{1,0:T(8,128)(2,1)} reduce(bf16[2048,1,128]{2,1,0:T(2,128)(2,1)S(1)} %bitcast.625, bf16[]{:T(256)} %broadcast.544), dimensions={1}, to_apply=%bitcast.394.reduce_sub_computation | reduce | bytes 1048578
  543.5 136.7 %while.82 = (s32[]{:T(128)}, f32[2048,2,64]{0,2,1:T(8,128)S(1)}, f32[2048,2,64]{0,2,1:T(8,128)}, bf16[4,512,2,64]{1,3,2,0:T(8,128)(2,1)}, s32[4]{0:T(128)S(1)}, ...) while((s32[]{:T(128)}, f32[2048,2,64]{0,2,1:T(8,128)S(1)}, ...), condition=%wide.region_17.18_spmd.clone, body=%wide.region_15.17_spmd.clone.sunk | while | flops 1377893888 | bytes 132430696 | solution.py:142
  545.9 5.7 fusion.328
  554.1 6.8 multiply_reduce_fusion.6
  579.8 5.7 fusion.328
  588.0 6.7 multiply_reduce_fusion.6
  614.0 5.7 fusion.328
  622.3 6.8 multiply_reduce_fusion.6
  656.5 6.8 multiply_reduce_fusion.6
  683.6 12.6 %reduce.19 = bf16[2048,128]{1,0:T(8,128)(2,1)S(1)} reduce(bf16[2048,1,128]{2,1,0:T(2,128)(2,1)} %bitcast.626, bf16[]{:T(256)} %broadcast.544), dimensions={1}, to_apply=%bitcast.402.reduce_sub_computation | reduce | bytes 1048578
  716.7 12.6 %reduce.22 = bf16[2048,128]{1,0:T(8,128)(2,1)S(1)} reduce(bf16[2048,1,128]{2,1,0:T(2,128)(2,1)} %bitcast.627, bf16[]{:T(256)} %broadcast.544), dimensions={1}, to_apply=%bitcast.390.reduce_sub_computation | reduce | bytes 1048578
  746.3 13.4 %reduce.21 = bf16[2048,128]{1,0:T(8,128)(2,1)} reduce(bf16[2048,1,128]{2,1,0:T(2,128)(2,1)} %bitcast.628, bf16[]{:T(256)} %broadcast.544), dimensions={1}, to_apply=%bitcast.392.reduce_sub_computation | reduce | bytes 1048578
  778.2 12.6 %reduce.18 = bf16[2048,128]{1,0:T(8,128)(2,1)S(1)} reduce(bf16[2048,1,128]{2,1,0:T(2,128)(2,1)} %bitcast.629, bf16[]{:T(256)} %broadcast.544), dimensions={1}, to_apply=%bitcast.398.reduce_sub_computation | reduce | bytes 1048578
  800.5 11.6 %reduce.17 = bf16[2048,128]{1,0:T(8,128)(2,1)S(1)} reduce(bf16[2048,1,128]{2,1,0:T(2,128)(2,1)S(1)} %bitcast.615, bf16[]{:T(256)} %broadcast.544), dimensions={1}, to_apply=%bitcast.400.reduce_sub_computation | reduce | bytes 1048578
  886.1 41.6 %all-reduce = (f32[512]{0:T(512)}, f32[512]{0:T(512)}) all-reduce(f32[512]{0:T(512)S(1)} %add.457, f32[512]{0:T(512)S(1)} %add.458), channel_id=1, replica_groups=mesh['dp'=8,'seq'=4] {'dp','seq'}, use_global_device_ids=true, to_apply=%region_26.27 | all-reduce | flops 1024 | bytes 8192 | tf_op jit(solution)/shard_map/psum | solution.py:324
  927.7 182.4 %all-reduce.4.cloned.1.call-done = (f32[512,512]{1,0:T(8,128)}, f32[512,512]{1,0:T(8,128)}, f32[512,512]{1,0:T(8,128)}, f32[512,512]{1,0:T(8,128)}, f32[512,1376...) async-done(((f32[512,512]{1,0:T(8,128)}, f32[512,512]{1,0:T(8,128)}, f32[512,512]{1,0:T(8,128)}, f32[512,512]{1,0:T(8,128)}, f32[512,1376]{0,1:T(8,128)}, ...) | async-done | bytes 12648464 | tf_op jit(solution)/shard_map/psum | solution.py:324
  (696 shorter events, 639.2 us)
Async XLA Ops:
  7.2 296.4 %copy-start = (bf16[1376,512]{1,0:T(8,128)(2,1)S(1)}, bf16[1376,512]{1,0:T(8,128)(2,1)}, u32[]{:S(2)}) copy-start(bf16[1376,512]{1,0:T(8,128)(2,1)} %param.31) | copy-start | bytes 4227076
  9.6 43.3 %copy-start.4 = (bf16[1,512,512]{1,2,0:T(8,128)(2,1)}, bf16[1,512,512]{1,2,0:T(8,128)(2,1)S(1)}, u32[]{:S(2)}) copy-start(bf16[1,512,512]{1,2,0:T(8,128)(2,1)S(1)} %copy.497) | copy-start | bytes 1572868
  9.8 43.2 %copy-start.107 = (f32[512]{0:T(512)}, f32[512]{0:T(512)S(1)}, u32[]{:S(2)}) copy-start(f32[512]{0:T(512)S(1)} %add_rsqrt_fusion.3) | copy-start | bytes 6148
  27.7 21.1 %all-to-all-start.1 = ((bf16[4,2,32768]{2,1,0:T(2,128)(2,1)}), bf16[4,2,32768]{2,1,0:T(2,128)(2,1)}, u32[]{:S(2)}, u32[]{:S(2)}) async-start(bf16[4,2,32768]{2,1,0:T(2,128)(2,1)} %reshape.1202), calls=%async_computation.1 | async-start | bytes 1048576 | tf_op jit(solution)/shard_map/all_to_all | solution.py:175
  48.8 18.2 %all-to-all-start = ((bf16[4,2,32768]{2,1,0:T(2,128)(2,1)}), bf16[4,2,32768]{2,1,0:T(2,128)(2,1)}, u32[]{:S(2)}, u32[]{:S(2)}) async-start(bf16[4,2,32768]{2,1,0:T(2,128)(2,1)} %reshape.1200), calls=%async_computation | async-start | bytes 1048576 | tf_op jit(solution)/shard_map/all_to_all | solution.py:174
  61.8 46.5 %copy-start.7 = (bf16[1,512,512]{1,2,0:T(8,128)(2,1)}, bf16[1,512,512]{1,2,0:T(8,128)(2,1)S(1)}, u32[]{:S(2)}) copy-start(bf16[1,512,512]{1,2,0:T(8,128)(2,1)S(1)} %copy.498) | copy-start | bytes 1572868
  61.9 46.3 %copy-start.105 = (f32[512]{0:T(512)}, f32[512]{0:T(512)S(1)}, u32[]{:S(2)}) copy-start(f32[512]{0:T(512)S(1)} %add_rsqrt_fusion.1) | copy-start | bytes 6148
  67.0 17.6 %all-to-all-start.2 = ((bf16[4,2,32768]{2,1,0:T(2,128)(2,1)}), bf16[4,2,32768]{2,1,0:T(2,128)(2,1)S(1)}, u32[]{:S(2)}, u32[]{:S(2)}) async-start(bf16[4,2,32768]{2,1,0:T(2,128)(2,1)} %reshape.1204), calls=%async_computation.2 | async-start | bytes 1048576 | tf_op jit(solution)/shard_map/all_to_all | solution.py:176
  85.4 17.4 %all-to-all-start.4 = ((bf16[4,2,32768]{2,1,0:T(2,128)(2,1)}), bf16[4,2,32768]{2,1,0:T(2,128)(2,1)S(1)}, u32[]{:S(2)}, u32[]{:S(2)}) async-start(bf16[4,2,32768]{2,1,0:T(2,128)(2,1)} %reshape.1192), calls=%async_computation.4 | async-start | bytes 1048576 | tf_op jit(solution)/shard_map/all_to_all | solution.py:174
  103.7 30.4 %all-to-all-start.5 = ((bf16[4,2,32768]{2,1,0:T(2,128)(2,1)}), bf16[4,2,32768]{2,1,0:T(2,128)(2,1)}, u32[]{:S(2)}, u32[]{:S(2)}) async-start(bf16[4,2,32768]{2,1,0:T(2,128)(2,1)} %reshape.1194), calls=%async_computation.5 | async-start | bytes 1048576 | tf_op jit(solution)/shard_map/all_to_all | solution.py:175
  108.2 11.8 %copy-start.55 = (bf16[2,512,512]{2,1,0:T(8,128)(2,1)S(1)}, bf16[2,512,512]{2,1,0:T(8,128)(2,1)}, u32[]{:S(2)}) copy-start(bf16[2,512,512]{2,1,0:T(8,128)(2,1)} %param.22) | copy-start | bytes 3145732
  134.0 76.2 %all-to-all-start.6 = ((bf16[4,2,32768]{2,1,0:T(2,128)(2,1)}), bf16[4,2,32768]{2,1,0:T(2,128)(2,1)S(1)}, u32[]{:S(2)}, u32[]{:S(2)}) async-start(bf16[4,2,32768]{2,1,0:T(2,128)(2,1)} %reshape.1196), calls=%async_computation.6 | async-start | bytes 1048576 | tf_op jit(solution)/shard_map/all_to_all | solution.py:176
  186.7 17.4 %copy-start.84 = (s32[1,2048]{1,0:T(1,128)}, s32[1,2048]{1,0:T(1,128)S(1)}, u32[]{:S(2)}) copy-start(s32[1,2048]{1,0:T(1,128)S(1)} %get-tuple-element.1219) | copy-start | bytes 24580
  186.7 17.4 %copy-start.109 = (f32[4,2,512]{2,1,0:T(2,128)}, f32[4,2,512]{2,1,0:T(2,128)S(1)}, u32[]{:S(2)}) copy-start(f32[4,2,512]{2,1,0:T(2,128)S(1)} %get-tuple-element.1081) | copy-start | bytes 49156
  186.7 16.9 %copy-start.68 = (bf16[4,2,32768]{2,1,0:T(2,128)(2,1)S(1)}, bf16[4,2,32768]{2,1,0:T(2,128)(2,1)}, u32[]{:S(2)}) copy-start(bf16[4,2,32768]{2,1,0:T(2,128)(2,1)} %copy-done.67) | copy-start | bytes 1572868
  211.0 77.6 %all-to-all-start.3 = ((bf16[4,2,32768]{2,1,0:T(2,128)(2,1)}), bf16[4,2,32768]{2,1,0:T(2,128)(2,1)}, u32[]{:S(2)}, u32[]{:S(2)}) async-start(bf16[4,2,32768]{2,1,0:T(2,128)(2,1)} %reshape.1206), calls=%async_computation.3 | async-start | bytes 1048576 | tf_op jit(solution)/shard_map/all_to_all | solution.py:184
  288.5 10.5 copy-start.5
  288.5 21.8 %all-to-all-start.7 = ((bf16[4,2,32768]{2,1,0:T(2,128)(2,1)}), bf16[4,2,32768]{2,1,0:T(2,128)(2,1)}, u32[]{:S(2)}, u32[]{:S(2)}) async-start(bf16[4,2,32768]{2,1,0:T(2,128)(2,1)} %reshape.1198), calls=%async_computation.7 | async-start | bytes 1048576 | tf_op jit(solution)/shard_map/all_to_all | solution.py:184
  331.6 11.5 %copy-start.45 = (bf16[1,4,512,128]{2,1,3,0:T(4,128)(2,1)S(1)}, bf16[1,4,512,128]{2,1,3,0:T(4,128)(2,1)}, u32[]{:S(2)}) copy-start(bf16[1,4,512,128]{2,1,3,0:T(4,128)(2,1)} %copy-done.44) | copy-start | bytes 1572868
  338.0 29.1 %all-to-all-start.12 = ((bf16[4,2,32768]{2,1,0:T(2,128)(2,1)}), bf16[4,2,32768]{2,1,0:T(2,128)(2,1)}, u32[]{:S(2)}, u32[]{:S(2)}) async-start(bf16[4,2,32768]{2,1,0:T(2,128)(2,1)} %reshape.1208), calls=%async_computation.12 | async-start | bytes 1048576 | tf_op jit(solution)/shard_map/all_to_all | solution.py:212
  344.2 11.1 copy-start.15
  367.0 166.2 %all-to-all-start.8 = ((bf16[4,2,32768]{2,1,0:T(2,128)(2,1)}), bf16[4,2,32768]{2,1,0:T(2,128)(2,1)}, u32[]{:S(2)}, u32[]{:S(2)}) async-start(bf16[4,2,32768]{2,1,0:T(2,128)(2,1)} %reshape.1216), calls=%async_computation.8 | async-start | bytes 1048576 | tf_op jit(solution)/shard_map/all_to_all | solution.py:212
  533.2 163.9 %all-to-all-start.15 = ((bf16[4,2,32768]{2,1,0:T(2,128)(2,1)}), bf16[4,2,32768]{2,1,0:T(2,128)(2,1)}, u32[]{:S(2)}, u32[]{:S(2)}) async-start(bf16[4,2,32768]{2,1,0:T(2,128)(2,1)} %reshape.1214), calls=%async_computation.15 | async-start | bytes 1048576 | tf_op jit(solution)/shard_map/all_to_all | solution.py:232
  681.5 20.7 %copy-start.28 = (bf16[512,512]{0,1:T(8,128)(2,1)S(1)}, bf16[512,512]{0,1:T(8,128)(2,1)}, u32[]{:S(2)}) copy-start(bf16[512,512]{0,1:T(8,128)(2,1)} %copy-done.27) | copy-start | bytes 1572868
  697.2 33.0 %all-to-all-start.11 = ((bf16[4,2,32768]{2,1,0:T(2,128)(2,1)}), bf16[4,2,32768]{2,1,0:T(2,128)(2,1)}, u32[]{:S(2)}, u32[]{:S(2)}) async-start(bf16[4,2,32768]{2,1,0:T(2,128)(2,1)} %reshape.1222), calls=%async_computation.11 | async-start | bytes 1048576 | tf_op jit(solution)/shard_map/all_to_all | solution.py:232
  730.2 31.6 %all-to-all-start.13 = ((bf16[4,2,32768]{2,1,0:T(2,128)(2,1)}), bf16[4,2,32768]{2,1,0:T(2,128)(2,1)}, u32[]{:S(2)}, u32[]{:S(2)}) async-start(bf16[4,2,32768]{2,1,0:T(2,128)(2,1)} %reshape.1210), calls=%async_computation.13 | async-start | bytes 1048576 | tf_op jit(solution)/shard_map/all_to_all | solution.py:218
  742.7 24.4 %copy-start.19 = (f32[1,512,512]{1,2,0:T(8,128)S(1)}, f32[1,512,512]{1,2,0:T(8,128)}, u32[]{:S(2)}) copy-start(f32[1,512,512]{1,2,0:T(8,128)} %copy-done.18) | copy-start | bytes 3145732
  761.7 30.0 %all-to-all-start.14 = ((bf16[4,2,32768]{2,1,0:T(2,128)(2,1)}), bf16[4,2,32768]{2,1,0:T(2,128)(2,1)}, u32[]{:S(2)}, u32[]{:S(2)}) async-start(bf16[4,2,32768]{2,1,0:T(2,128)(2,1)} %reshape.1212), calls=%async_computation.14 | async-start | bytes 1048576 | tf_op jit(solution)/shard_map/all_to_all | solution.py:225
  791.7 35.5 %all-to-all-start.9 = ((bf16[4,2,32768]{2,1,0:T(2,128)(2,1)}), bf16[4,2,32768]{2,1,0:T(2,128)(2,1)}, u32[]{:S(2)}, u32[]{:S(2)}) async-start(bf16[4,2,32768]{2,1,0:T(2,128)(2,1)} %reshape.1218), calls=%async_computation.9 | async-start | bytes 1048576 | tf_op jit(solution)/shard_map/all_to_all | solution.py:218
  827.3 13.7 %copy-start.21 = (f32[1,512,4,128]{1,3,2,0:T(8,128)}, f32[1,512,4,128]{1,3,2,0:T(8,128)S(1)}, u32[]{:S(2)}) copy-start(f32[1,512,4,128]{1,3,2,0:T(8,128)S(1)} %copy.456) | copy-start | bytes 3145732
  827.3 18.6 %all-to-all-start.10 = ((bf16[4,2,32768]{2,1,0:T(2,128)(2,1)}), bf16[4,2,32768]{2,1,0:T(2,128)(2,1)}, u32[]{:S(2)}, u32[]{:S(2)}) async-start(bf16[4,2,32768]{2,1,0:T(2,128)(2,1)} %reshape.1220), calls=%async_computation.10 | async-start | bytes 1048576 | tf_op jit(solution)/shard_map/all_to_all | solution.py:225
  832.4 277.7 %all-reduce.4.cloned.1.call-start = ((), (), s32[]{:S(2)}) async-start(), calls=%async_computation.16 | async-start | bytes 25296896 | tf_op jit(solution)/shard_map/psum | solution.py:324
  (123 other events, 441.7 us)
Sparse Core Ops, SparseCore 0:
  867.9 242.1 all-reduce.3
where the time goes:
time: 1140 us; the launch traced here: 1130 us
  matrix products  314 us (28%)
  other arithmetic  235 us (21%)
  local copies, waits for them, and re-layouts  205 us (18%)
  waiting for transfers between devices  200 us (18%)
  starting transfers between devices  80.2 us (7%)
  blocking collectives  41.6 us (4%)
  loops' own time  37 us (3%)
  between operations  16.1 us (1%)
    psum x1, waiting for transfers between devices, on_device(): lax.psum((sum_ga, sum_gm, sum_wq, sum_wk, sum_wv, sum_wo, sum_wg, sum_wu,...  182 us
    unnamed x20, other arithmetic  135 us
    unnamed x278, local copies, waits for them, and re-layouts  102 us
    dot_general x16, matrix products, masked_scores(): jnp.einsum('qhd,khd->hqk', block_query, key_rows, preferred_element_type=...  69.2 us
    dot_general x8, matrix products, step_block(): jnp.einsum('qhd,khd->hqk', block_grad, value_rows, preferred_element_type...  54 us
    psum x1, blocking collectives, on_device(): lax.psum((sum_ga, sum_gm, sum_wq, sum_wk, sum_wv, sum_wo, sum_wg, sum_wu,...  41.6 us
    dot_general x8, matrix products, step_block(): jnp.einsum('hqk,qhd->khd', weights_low, block_grad, preferred_element_typ...  38.4 us
    dot_general x28, matrix products, flat_dot(): return jnp.dot(left, right, preferred_element_type=jnp.float32)  37.4 us
  transfers between devices with their start and end apart: 17, of which 5 were waited for; matrix products, arithmetic and copies ran while one was open for 59% of the time, Pallas kernels for 0%

commit v1 on v0

v1 whole, which is shorter than its diff:
```python
import functools

import jax
import jax.numpy as jnp
from jax import lax
from jax.experimental import pallas as pl
from jax.experimental.pallas import tpu as pltpu
from jax.sharding import PartitionSpec as P

HD = 64
DOCS = 7
epsilon = 1e-05
theta_base = 10000.0
masked_value = -1e30
MESH = pl.DeviceIdType.MESH
f32 = jnp.float32
bf16 = jnp.bfloat16
QB = 256
MB = 256


def dot(left, right, left_dim, right_dim):
    return lax.dot_general(
        left, right, (((left_dim,), (right_dim,)), ((), ())), preferred_element_type=f32
    )


def strip_offset(block):
    return QB * block * (block + 1) // 2


def fold_rows(values):
    rows, width = values.shape
    return jnp.sum(values.reshape(rows // 8, 8, width), axis=0)


def block_kernel(
    G, S, T, L, D, FF,
    x, seg, cot, gain_a, gain_m, wq, wk, wv, wo, wg, wu, wd,
    out, gin, g_ga, g_gm, g_qkv, g_out, g_gate, g_up, g_down,
    xs, cots, seg_other, first_s, cos_s, sin_s, n_s, wqkv, wqkvT, wo_s, wg_s, wu_s, wd_s,
    qTz, k_s, kT, v_s, vT, p_s, inv_tot, mixT, mfull, mid, nm, hid, dga, dup, da, dmT, outb,
    dO_in, dOz, dacc_k, dacc_v, dn_in,
    w_sem, loc_sem, seg_sem, x_send, x_recv, fwd_send, cot_send, cot_recv, mix_send, mix_recv,
    out_send, out_recv, dm_send, dm_recv, dn_send, dn_recv, gin_send, gin_recv, g_sem,
):
    d = lax.axis_index("dp")
    z = lax.axis_index("seq")
    c = lax.rem(d, 2)
    pair = d - c
    sib = pair + 1 - c
    gz = z // G
    lz = lax.rem(z, G)
    half = L // 2
    Dh = D // 2
    NH = Dh // HD

    def remote(src, dst, send, recv, dp, seq):
        return pltpu.make_async_remote_copy(
            src_ref=src, dst_ref=dst, send_sem=send, recv_sem=recv,
            device_id=(dp, seq), device_id_type=MESH,
        )

    loads = [
        pltpu.make_async_copy(w.at[:, pl.ds(pl.multiple_of(c * Dh, Dh), Dh)], wqkv.at[i], w_sem.at[i])
        for i, w in enumerate((wq, wk, wv))
    ] + [
        pltpu.make_async_copy(w, s, w_sem.at[3 + i])
        for i, (w, s) in enumerate(((wo, wo_s), (wg, wg_s), (wu, wu_s), (wd, wd_s)))
    ]
    for load in loads:
        load.start()

    barrier = pltpu.get_barrier_semaphore()
    for step in range(1, 2 * S):
        other = lax.rem(c * S + z + step, 2 * S)
        pl.semaphore_signal(
            barrier, inc=1, device_id=(pair + other // S, lax.rem(other, S)), device_id_type=MESH
        )
    pl.semaphore_wait(barrier, 2 * S - 1)

    seg_copy = remote(seg, seg_other, seg_sem.at[0], seg_sem.at[1], sib, z)
    seg_copy.start()

    def x_rows(index):
        return xs.at[pl.ds(pl.multiple_of(index * T, T), T)]

    def x_copy(l):
        return remote(x.at[l], x_rows(z), x_send.at[l], x_recv.at[z], d, c * G + l)

    own_x = pltpu.make_async_copy(x.at[lz], x_rows(z), loc_sem.at[0])
    own_fwd = remote(x.at[lz], x_rows(z), fwd_send.at[0], x_recv.at[z], sib, z)

    @pl.when(gz == c)
    def _():
        own_x.start()
        own_fwd.start()

    for l in range(G):
        @pl.when(c * G + l != z)
        def _():
            x_copy(l).start()

    for load in loads:
        load.wait()
    for i in range(3):
        wqkvT[i * Dh:(i + 1) * Dh, :] = wqkv[i].T
    seg_copy.wait()
    seg_mine = jnp.where(gz == c, seg[...], seg_other[...])
    row = jnp.zeros((1, L), jnp.int32)
    for l in range(G):
        row = jnp.where(lz == l, seg_mine[l:l + 1, :], row)
    ids = row.astype(f32)
    first = jnp.zeros((1, L), f32)
    for doc in range(1, DOCS):
        before = jnp.sum(jnp.where(ids < doc, 1.0, 0.0), axis=1, keepdims=True)
        first = jnp.where(ids >= doc, before, first)
    first_s[...] = jnp.broadcast_to(first, (8, L))
    token = lax.broadcasted_iota(jnp.int32, (1, L), 1).astype(f32)
    place = token - first
    order = lax.broadcasted_iota(jnp.int32, (HD // 2, 1), 0).astype(f32)
    frequency = jnp.exp(order * f32(-2.0 * 9.210340371976184 / HD))
    angle = place * frequency
    cos_s[...] = jnp.cos(angle)
    sin_s[...] = jnp.sin(angle)

    def rms(values):
        inverse = lax.rsqrt(jnp.mean(values * values, axis=-1, keepdims=True) + epsilon)
        return values * inverse, inverse

    def project(start, size):
        rows = pl.ds(start, size)
        plain, _ = rms(xs[rows, :].astype(f32))
        normed = (plain * gain_a[...]).astype(bf16)
        n_s[rows, :] = normed
        lin = dot(wqkvT[...], normed, 1, 1)
        cosine, sine = cos_s[:, rows], sin_s[:, rows]

        def rotated(base, scale):
            parts = []
            for h in range(NH):
                a = lin[base + h * HD:base + h * HD + HD // 2]
                b = lin[base + h * HD + HD // 2:base + (h + 1) * HD]
                parts.append(jnp.concatenate([a * cosine - b * sine, b * cosine + a * sine], axis=0))
            return parts

        zeros = jnp.zeros((HD, size), bf16)
        for h, q in enumerate(rotated(0, 1.0)):
            q = (q.astype(bf16).astype(f32) * HD ** -0.5).astype(bf16)
            qTz[h, :, rows] = jnp.concatenate([q, zeros] if h % 2 == 0 else [zeros, q], axis=0)
        keys = jnp.concatenate(rotated(Dh, 1.0), axis=0).astype(bf16)
        kT[:, rows] = keys
        k_s[rows, :] = keys.T
        values = lin[2 * Dh:].astype(bf16)
        vT[:, rows] = values
        v_s[rows, :] = values.T

    for step in range(S):
        source = lax.rem(z + step, S)
        arrived = remote(x.at[0], x_rows(source), x_send.at[0], x_recv.at[source], sib, z)
        if step == 0:
            @pl.when(gz == c)
            def _():
                own_x.wait()

            @pl.when(gz != c)
            def _():
                arrived.wait_recv()
        else:
            arrived.wait_recv()

            @pl.when(gz == c)
            def _():
                remote(x_rows(source), x_rows(source), fwd_send.at[step], x_recv.at[source], sib, z).start()

        @pl.loop(0, T // QB)
        def _(i):
            project(pl.multiple_of(source * T + i * QB, QB), QB)

    for l in range(G):
        @pl.when(c * G + l != z)
        def _():
            x_copy(l).wait_send()

    @pl.when(gz == c)
    def _():
        own_fwd.wait_send()
        for step in range(1, S):
            remote(x.at[0], x_rows(z), fwd_send.at[step], x_recv.at[z], sib, z).wait_send()

    to_core = z // G
    slot = lax.rem(z, G)

    def cot_rows(index):
        return cots.at[pl.ds(pl.multiple_of(index * T, T), T)]

    def cot_copy(l):
        return remote(cot.at[l], cot_rows(slot), cot_send.at[l], cot_recv.at[slot], pair + to_core, c * G + l)

    own_cot = pltpu.make_async_copy(cot.at[lz], cot_rows(slot), loc_sem.at[1])
    keeps_own = (gz == c) & (to_core == c)
    for l in range(G):
        here = (c * G + l == z) & (to_core == c)

        @pl.when(jnp.logical_not(here))
        def _():
            cot_copy(l).start()

    @pl.when(keeps_own)
    def _():
        own_cot.start()

    def mask_of(strip_rows, qb, s, row0):
        j = (lax.broadcasted_iota(jnp.int32, (strip_rows, QB), 0) + row0).astype(f32)
        i = (lax.broadcasted_iota(jnp.int32, (1, QB), 1) + qb * QB).astype(f32)
        begin = first_s[0:1, qb * QB:(qb + 1) * QB]
        return jnp.where((j >= begin) & (j <= i), s, masked_value)

    def mix_copy(h):
        return remote(
            mixT.at[pl.ds(pl.multiple_of(h * HD, HD), HD), pl.ds(pl.multiple_of((1 - c) * half, half), half)],
            mfull.at[pl.ds(pl.multiple_of(c * Dh + h * HD, HD), HD), :],
            mix_send.at[h], mix_recv.at[h], sib, z,
        )

    NQ = L // QB

    @pl.loop(0, NH)
    def _(h):
        rows = pl.ds(pl.multiple_of(h * HD, HD), HD)
        lanes = pl.ds(pl.multiple_of((h // 2) * 2 * HD, 2 * HD), 2 * HD)
        for qb in range(NQ):
            cols = slice(qb * QB, (qb + 1) * QB)
            depth = (qb + 1) * QB
            s = dot(k_s[0:depth, lanes], qTz[h, :, cols], 1, 0)
            if qb == NQ - 1:
                s = mask_of(depth, qb, s, 0)
            elif qb < 2:
                s = mask_of(depth, qb, s, 0)
            else:
                s = jnp.concatenate(
                    [mask_of(QB, qb, s[:QB], 0), s[QB:depth - QB], mask_of(QB, qb, s[depth - QB:], depth - QB)],
                    axis=0,
                )
            top = jnp.max(s, axis=0, keepdims=True)
            expanded = jnp.exp(s - top)
            inverse = 1.0 / jnp.sum(expanded, axis=0, keepdims=True)
            low = expanded.astype(bf16)
            p_s[h, strip_offset(qb):strip_offset(qb) + depth, :] = low
            inv_tot[h, :, cols] = jnp.broadcast_to(inverse, (8, QB))
            mixT[rows, cols] = (dot(vT[rows, 0:depth], low, 1, 0) * inverse).astype(bf16)
        mix_copy(h).start()
        mfull[pl.ds(pl.multiple_of(c * Dh + h * HD, HD), HD), :] = mixT[
            rows, pl.ds(pl.multiple_of(c * half, half), half)
        ]

    @pl.loop(0, NH)
    def _(h):
        mix_copy(h).wait_send()
        remote(
            mixT.at[0:HD, 0:half], mfull.at[pl.ds(pl.multiple_of((1 - c) * Dh + h * HD, HD), HD), :],
            mix_send.at[h], mix_recv.at[h], sib, z,
        ).wait_recv()

    for l in range(G):
        here = (c * G + l == z) & (to_core == c)

        @pl.when(jnp.logical_not(here))
        def _():
            cot_copy(l).wait_send()

    for j in range(G):
        mine = (gz == c) & (c * G + j == z)

        @pl.when(jnp.logical_not(mine))
        def _():
            remote(cot.at[0], cot_rows(j), cot_send.at[0], cot_recv.at[j], sib, z).wait_recv()

    @pl.when(keeps_own)
    def _():
        own_cot.wait()

    middle_col = (FF // 2 + 255) // 256 * 256
    ff_cuts = ((0, middle_col), (middle_col, FF))
    g_gm[...] = jnp.zeros((8, D), f32)

    @pl.loop(0, half // MB)
    def _(i):
        start = pl.multiple_of(i * MB, MB)
        rows = pl.ds(start, MB)
        base = xs[pl.ds(pl.multiple_of(c * half + start, MB), MB), :].astype(f32)
        middle = base + dot(mfull[:, rows], wo_s[...], 0, 0)
        plain, inverse = rms(middle)
        gain = gain_m[...]
        normed = (plain * gain).astype(bf16)
        nm[rows, :] = normed
        grad = cots[rows, :]
        result = middle
        d_normed = None
        for first_col, last_col in ff_cuts:
            cut = slice(first_col, last_col)
            gate = dot(normed, wg_s[:, cut], 1, 0)
            up = dot(normed, wu_s[:, cut], 1, 0)
            sig = 1.0 / (1.0 + jnp.exp(-gate))
            act = gate * sig
            hidden = (act * up).astype(bf16)
            hid[rows, cut] = hidden
            result = result + dot(hidden, wd_s[cut, :], 1, 0)
            d_hidden = dot(grad, wd_s[cut, :], 1, 1)
            d_gate = (d_hidden * up * sig * (1.0 + gate * (1.0 - sig))).astype(bf16)
            d_up = (d_hidden * act).astype(bf16)
            dga[rows, cut] = d_gate
            dup[rows, cut] = d_up
            term = dot(d_gate, wg_s[:, cut], 1, 1) + dot(d_up, wu_s[:, cut], 1, 1)
            d_normed = term if d_normed is None else d_normed + term
        outb[rows, :] = result.astype(bf16)
        scaled = d_normed * gain
        g_gm[...] += fold_rows(d_normed * plain)
        d_middle = grad.astype(f32) + inverse * (scaled - plain * jnp.mean(scaled * plain, axis=-1, keepdims=True))
        mid[rows, :] = d_middle
        d_attn = d_middle.astype(bf16)
        da[rows, :] = d_attn
        dmT[:, rows] = dot(wo_s[...], d_attn, 1, 1).astype(bf16)

    dm_copy = remote(
        dmT.at[pl.ds(pl.multiple_of((1 - c) * Dh, Dh), Dh), :], dO_in, dm_send.at[0], dm_recv.at[0], sib, z
    )
    dm_copy.start()

    def back_copy(j, src, dst, send, recv):
        return remote(src.at[pl.ds(j * T, T)], dst.at[lz], send.at[j], recv.at[lz], pair + gz, c * G + j)

    def back_start(src, dst, send, recv, local):
        for j in range(G):
            mine = (gz == c) & (c * G + j == z)

            @pl.when(jnp.logical_not(mine))
            def _():
                back_copy(j, src, dst, send, recv).start()

            @pl.when(mine)
            def _():
                pltpu.make_async_copy(src.at[pl.ds(j * T, T)], dst.at[lz], local).start()

    def back_wait(src, dst, send, recv, local):
        for j in range(G):
            mine = (gz == c) & (c * G + j == z)

            @pl.when(jnp.logical_not(mine))
            def _():
                back_copy(j, src, dst, send, recv).wait_send()

            @pl.when(mine)
            def _():
                pltpu.make_async_copy(src.at[pl.ds(j * T, T)], dst.at[lz], local).wait()
        for l in range(G):
            mine = (c * G + l == z) & (z // G == c)

            @pl.when(jnp.logical_not(mine))
            def _():
                remote(src.at[pl.ds(0, T)], dst.at[l], send.at[0], recv.at[l], sib, z).wait_recv()

    back_start(outb, out, out_send, out_recv, loc_sem.at[2])

    wg_s[...] = dot(nm[...], dga[...], 0, 0).astype(bf16)
    wu_s[...] = dot(nm[...], dup[...], 0, 0).astype(bf16)
    wd_s[...] = dot(hid[...], cots[...], 0, 0).astype(bf16)
    wo_s[...] = dot(mfull[...], da[...], 1, 0).astype(bf16)
    copies = [
        pltpu.make_async_copy(wg_s, g_gate, g_sem.at[0]),
        pltpu.make_async_copy(wu_s, g_up, g_sem.at[1]),
        pltpu.make_async_copy(wd_s, g_down, g_sem.at[2]),
        pltpu.make_async_copy(wo_s, g_out, g_sem.at[3]),
    ]
    for copy in copies:
        copy.start()

    dm_copy.wait()

    def take(values, offset):
        tokens = values.shape[1]
        zeros = jnp.zeros((HD, tokens), bf16)
        for h in range(NH):
            inverse = inv_tot[h, 0:1, pl.ds(offset, tokens)]
            grad = (values[h * HD:(h + 1) * HD].astype(f32) * inverse).astype(bf16)
            dOz[h, :, pl.ds(offset, tokens)] = jnp.concatenate(
                [grad, zeros] if h % 2 == 0 else [zeros, grad], axis=0
            )

    take(dmT[pl.ds(pl.multiple_of(c * Dh, Dh), Dh), :], pl.multiple_of(c * half, half))
    take(dO_in[...], pl.multiple_of((1 - c) * half, half))

    parts = (dga, dup, hid)

    def unrotated(values, cosine, sine):
        a, b = values[:HD // 2], values[HD // 2:]
        return jnp.concatenate([a * cosine + b * sine, b * cosine - a * sine], axis=0)

    @pl.loop(0, NH)
    def _(h):
        rows = pl.ds(pl.multiple_of(h * HD, HD), HD)
        lanes = pl.ds(pl.multiple_of((h // 2) * 2 * HD, 2 * HD), 2 * HD)
        inner = pl.ds(pl.multiple_of(lax.rem(h, 2) * HD, HD), HD)
        for qb in reversed(range(NQ)):
            cols = slice(qb * QB, (qb + 1) * QB)
            depth = (qb + 1) * QB
            low = p_s[h, strip_offset(qb):strip_offset(qb) + depth, :]
            grad = dOz[h, inner, cols]
            delta = jnp.sum(grad.astype(f32) * mixT[rows, cols].astype(f32), axis=0, keepdims=True)
            d_probs = dot(v_s[0:depth, lanes], dOz[h, :, cols], 1, 0)
            d_scores = (low.astype(f32) * (d_probs - delta)).astype(bf16)
            add_v = dot(grad, low, 1, 1)
            add_k = dot(qTz[h, inner, cols], d_scores, 1, 1)
            if qb == NQ - 1:
                dacc_v[:, 0:depth] = add_v
                dacc_k[:, 0:depth] = add_k
            else:
                dacc_v[:, 0:depth] += add_v
                dacc_k[:, 0:depth] += add_k
            d_query = dot(kT[rows, 0:depth], d_scores, 1, 0) * HD ** -0.5
            side, lane = divmod(qb * QB, half)
            parts[0][pl.ds(pl.multiple_of(side * Dh + h * HD, HD), HD), lane:lane + QB] = unrotated(
                d_query.astype(bf16).astype(f32), cos_s[:, cols], sin_s[:, cols]
            ).astype(bf16)
        for side in range(2):
            cols = slice(side * half, (side + 1) * half)
            place_rows = pl.ds(pl.multiple_of(side * Dh + h * HD, HD), HD)
            parts[1][place_rows, 0:half] = unrotated(
                dacc_k[:, cols].astype(bf16).astype(f32), cos_s[:, cols], sin_s[:, cols]
            ).astype(bf16)
            parts[2][place_rows, 0:half] = dacc_v[:, cols].astype(bf16)

    back_wait(outb, out, out_send, out_recv, loc_sem.at[2])

    def back_norm(side, start):
        side_rows = pl.ds(pl.multiple_of(side * Dh, Dh), Dh)
        total = None
        for i in range(3):
            term = dot(parts[i][side_rows, pl.ds(start, MB)], wqkvT[i * Dh:(i + 1) * Dh, :], 0, 0)
            total = term if total is None else total + term
        return total

    @pl.loop(0, half // MB)
    def _(i):
        start = pl.multiple_of(i * MB, MB)
        da[pl.ds(start, MB), :] = back_norm(1 - c, start).astype(bf16)

    dn_copy = remote(da, dn_in, dn_send.at[0], dn_recv.at[0], sib, z)
    dn_copy.start()

    for i in range(3):
        grad = dot(parts[i][0:Dh, 0:half], n_s[0:half, :], 1, 0)
        grad = grad + dot(parts[i][Dh:2 * Dh, 0:half], n_s[half:L, :], 1, 0)
        wqkv[i] = grad.T.astype(bf16)
    copies.append(pltpu.make_async_copy(wqkv, g_qkv, g_sem.at[4]))
    copies[-1].start()
    dn_copy.wait()

    g_ga[...] = jnp.zeros((8, D), f32)

    @pl.loop(0, half // MB)
    def _(i):
        start = pl.multiple_of(i * MB, MB)
        rows = pl.ds(start, MB)
        own = pl.ds(pl.multiple_of(c * half + start, MB), MB)
        d_normed = back_norm(c, start) + dn_in[rows, :].astype(f32)
        plain, inverse = rms(xs[own, :].astype(f32))
        scaled = d_normed * gain_a[...]
        g_ga[...] += fold_rows(d_normed * plain)
        d_start = inverse * (scaled - plain * jnp.mean(scaled * plain, axis=-1, keepdims=True))
        nm[rows, :] = (mid[rows, :] + d_start).astype(bf16)

    back_start(nm, gin, gin_send, gin_recv, loc_sem.at[3])
    for copy in copies:
        copy.wait()
    back_wait(nm, gin, gin_send, gin_recv, loc_sem.at[3])


def on_device(
    G, S,
    inputs, segment_ids, cotangent, norm_attn, norm_mlp, w_query, w_key, w_value, w_out, w_gate, w_up, w_down,
):
    _, T, D = inputs.shape
    FF = w_gate.shape[1]
    L = T * S
    half, Dh = L // 2, D // 2
    NH = Dh // HD
    anywhere = pl.BlockSpec(memory_space=pl.ANY)
    vmem = pl.BlockSpec(memory_space=pltpu.VMEM)
    dma = pltpu.SemaphoreType.DMA

    def buf(*shape, dtype=bf16):
        return pltpu.VMEM(shape, dtype)

    strips = strip_offset(L // QB)
    outs = pl.pallas_call(
        functools.partial(block_kernel, G, S, T, L, D, FF),
        out_shape=[
            jax.ShapeDtypeStruct((G, T, D), bf16),
            jax.ShapeDtypeStruct((G, T, D), bf16),
            jax.ShapeDtypeStruct((8, D), f32),
            jax.ShapeDtypeStruct((8, D), f32),
            jax.ShapeDtypeStruct((3, D, Dh), bf16),
            jax.ShapeDtypeStruct((D, D), bf16),
            jax.ShapeDtypeStruct((D, FF), bf16),
            jax.ShapeDtypeStruct((D, FF), bf16),
            jax.ShapeDtypeStruct((FF, D), bf16),
        ],
        in_specs=[anywhere, vmem, anywhere, vmem, vmem] + [anywhere] * 7,
        out_specs=[anywhere, anywhere, vmem, vmem] + [anywhere] * 5,
        scratch_shapes=[
            buf(L, D), buf(half, D), buf(G, L, dtype=jnp.int32), buf(8, L, dtype=f32),
            buf(HD // 2, L, dtype=f32), buf(HD // 2, L, dtype=f32),
            buf(L, D), buf(3, D, Dh), buf(3 * Dh, D), buf(D, D), buf(D, FF), buf(D, FF), buf(FF, D),
            buf(NH, 2 * HD, L), buf(L, Dh), buf(Dh, L), buf(L, Dh), buf(Dh, L),
            buf(NH, strips, QB), buf(NH, 8, L, dtype=f32), buf(Dh, L), buf(D, half),
            buf(half, D, dtype=f32), buf(half, D), buf(half, FF), buf(half, FF), buf(half, FF),
            buf(half, D), buf(D, half), buf(half, D),
            buf(Dh, half), buf(NH, 2 * HD, L), buf(HD, L, dtype=f32), buf(HD, L, dtype=f32),
            buf(half, D),
            dma((7,)), dma((4,)), dma((2,)), dma((G,)), dma((S,)), dma((S,)), dma((G,)), dma((G,)),
            dma((NH,)), dma((NH,)), dma((G,)), dma((G,)), dma((1,)), dma((1,)), dma((1,)), dma((1,)),
            dma((G,)), dma((G,)), dma((5,)),
        ],
        compiler_params=pltpu.CompilerParams(
            collective_id=0, has_side_effects=True, vmem_limit_bytes=63 * 2**20
        ),
    )(
        inputs, segment_ids, cotangent, norm_attn.reshape(1, D), norm_mlp.reshape(1, D),
        w_query, w_key, w_value, w_out, w_gate, w_up, w_down,
    )
    out, gin, g_ga, g_gm, g_qkv, g_out, g_gate, g_up, g_down = outs
    c = lax.rem(lax.axis_index("dp"), 2)

    def whole(part):
        return lax.dynamic_update_slice(jnp.zeros((D, D), f32), part.astype(f32), (0, c * Dh))

    grads = (
        jnp.sum(g_ga, axis=0), jnp.sum(g_gm, axis=0),
        whole(g_qkv[0]), whole(g_qkv[1]), whole(g_qkv[2]),
        g_out.astype(f32), g_gate.astype(f32), g_up.astype(f32), g_down.astype(f32),
    )
    return (out, gin.astype(f32)) + tuple(lax.psum(grads, ("dp", "seq")))


def solution(mesh):
    S = mesh.shape["seq"]
    G = S // 2
    rows = P("dp", "seq", None)
    return jax.shard_map(
        functools.partial(on_device, G, S),
        mesh=mesh,
        in_specs=(rows, P("dp", None), rows) + (P(),) * 9,
        out_specs=(rows, rows) + (P(),) * 9,
        check_vma=False,
    )
```

time: 1140 us -> 353 us (0.31)
  matrix products: 314 us -> 0 us
  other arithmetic: 235 us -> 2.83 us
  waiting for transfers between devices: 200 us -> 0.02 us
  local copies, waits for them, and re-layouts: 205 us -> 18.8 us
  blocking collectives: 41.6 us -> 192 us
  Pallas kernels: 0 us -> 124 us
  starting transfers between devices: 80.2 us -> 0.04 us
  loops' own time: 37 us -> 0 us
    dot_general x98 -> x0, matrix products: 314 us -> none  [the longest x16 69.2 us: masked_scores(): jnp.einsum('qhd,khd->hqk', block_query, key_rows, preferred_element_type=...]
    psum x1, waiting for transfers between devices: 182 us -> 0.01 us  [on_device(): return (out, gin.astype(f32)) + tuple(lax.psum(grads, ('dp', 'seq')))]
    psum x1, blocking collectives: 41.6 us -> 192 us  [on_device(): return (out, gin.astype(f32)) + tuple(lax.psum(grads, ('dp', 'seq')))]
    unnamed x20 -> x0, other arithmetic: 135 us -> none
    pallas_call x0 -> x1, Pallas kernels: none -> 124 us  [on_device(): pl.pallas_call(functools.partial(block_kernel, G, S, T, L, D, FF), out_sh...]
    unnamed x278 -> x30, local copies, waits for them, and re-layouts: 102 us -> 18.4 us
    all_to_all x16 -> x0, starting transfers between devices: 80.2 us -> none  [the longest x2 11 us: layer_step(): lax.all_to_all(key_low, 'seq', split_axis=2, concat_axis=1, tiled=True)]
    convert_element_type x23 -> x1, other arithmetic: 49.9 us -> 1.61 us  [on_device(): return (out, gin.astype(f32)) + tuple(lax.psum(grads, ('dp', 'seq')))]
  transfers between devices with their start and end apart: 17 -> 1, of which waited for: 5 -> 0; matrix products, arithmetic and copies ran while one was open for 59% -> 2% of each run, Pallas kernels for 0% -> 0%
where the time goes in v1:
time: 353 us; the launch traced here: 352 us
  blocking collectives  192 us (54%)
  Pallas kernels  124 us (35%)
  local copies, waits for them, and re-layouts  18.8 us (5%)
  between operations  14.2 us (4%)
    psum x1, blocking collectives, on_device(): return (out, gin.astype(f32)) + tuple(lax.psum(grads, ('dp', 'seq')))  192 us
    pallas_call x1, Pallas kernels, on_device(): pl.pallas_call(functools.partial(block_kernel, G, S, T, L, D, FF), out_sh...  124 us
    unnamed x30, local copies, waits for them, and re-layouts  18.4 us
  transfers between devices with their start and end apart: 1, of which 0 were waited for; matrix products, arithmetic and copies ran while one was open for 2% of the time, Pallas kernels for 0%

profile of v1, /device:TPU:0, one launch (start us, length us, event | category | flops | bytes accessed | tf_op | source)
XLA Modules:
  0.0 352.1 jit_solution(16074513163086103574)
XLA Ops:
  7.2 0.0 copy-start.3
  7.2 0.0 all-reduce.5.cloned.1.call-start
  7.2 2.6 copy.23.wg
  9.9 0.0 copy-done.3
  9.9 1.5 copy.24.wu
  11.4 124.1 %shard_map.203 = (bf16[2,512,512]{2,1,0:T(8,128)(2,1)}, bf16[2,512,512]{2,1,0:T(8,128)(2,1)}, f32[8,512]{1,0:T(8,128)}, f32[8,512]{1,0:T(8,128)}, bf16[3,512,256...) custom-call(bf16[2,512,512]{2,1,0:T(8,128)(2,1)} %x.1, ...), custom_call_target="tpu_custom_call" | custom-call | tf_op jit(solution)/shard_map/pallas_call | solution.py:496
  135.5 0.0 copy-start.8
  135.5 0.1 broadcast.4.clone
  135.6 1.1 convert_dynamic-update-slice_fusion.2
  136.7 0.0 copy-start.1
  136.7 0.1 broadcast.4.clone.1
  136.8 0.0 copy-done.8
  136.8 0.1 convert_dynamic-update-slice_fusion.1
  136.9 0.0 copy-start.2
  136.9 0.1 broadcast.4.clone.2
  137.0 0.6 copy-done.1
  137.7 0.0 copy-start
  137.7 0.0 copy-start.4
  137.7 0.3 copy-done.2
  138.0 0.7 copy-done
  138.7 0.0 all-reduce.5.cloned.1.call-update
  138.7 0.6 copy-done.4
  139.3 1.6 convert_element_type.33
  141.0 192.2 %all-reduce.6 = (f32[512]{0:T(512)}, f32[512]{0:T(512)}, f32[512,512]{1,0:T(8,128)}, f32[512,1376]{1,0:T(8,128)}, f32[512,1376]{1,0:T(8,128)S(1)}, /*index=5*/f32[1376,512]{1,0:T(8,128)}) all-reduce(f32[512]{0:T(512)S(1)} %reduce_sum.18, f32[512]{0:T(512)S(1)} %reduce_sum.19, ...), channel_id=1, replica_groups=mesh['dp'=8,'seq'=4] {'dp','seq'}, use_global_device_ids=true, to_apply=%region_1.0 | all-reduce | flops 2376704 | bytes 14262272 | tf_op jit(solution)/shard_map/psum | solution.py:543
  333.2 3.3 copy.25
  336.5 2.2 copy.26
  338.7 2.4 copy.46
  341.0 1.0 copy.47
  342.0 0.6 copy-done.6
  342.7 1.0 copy.48
  343.6 0.6 copy-done.5
  344.3 1.0 copy.49
  (12 shorter events, 0.1 us)
Async XLA Ops:
  7.2 2.7 copy-start.3
  7.2 331.5 %all-reduce.5.cloned.1.call-start = ((), (), s32[]{:S(2)}) async-start(), calls=%async_computation | async-start | bytes 6291456 | tf_op jit(solution)/shard_map/psum | solution.py:543
  135.5 1.4 copy-start.8
  136.7 1.0 copy-start.1
  136.9 1.1 copy-start.2
  137.7 1.0 copy-start
  137.7 1.6 copy-start.4
  139.3 1.6 copy-start.10
  139.3 1.6 copy-start.9
  338.7 2.4 copy-start.7
  341.0 1.6 copy-start.6
  342.7 1.6 copy-start.5
Sparse Core Ops, SparseCore 0:
  138.8 153.9 all-reduce.4

commit v2 on v1

v2 whole, which is shorter than its diff:
```python
import functools

import jax
import jax.numpy as jnp
from jax import lax
from jax.experimental import pallas as pl
from jax.experimental.pallas import tpu as pltpu
from jax.sharding import PartitionSpec as P

HD = 64
DOCS = 7
epsilon = 1e-05
theta_base = 10000.0
masked_value = -1e30
MESH = pl.DeviceIdType.MESH
f32 = jnp.float32
bf16 = jnp.bfloat16
QB = 256
MB = 256
EDGE = 128


def dot(left, right, left_dim, right_dim):
    return lax.dot_general(
        left, right, (((left_dim,), (right_dim,)), ((), ())), preferred_element_type=f32
    )


def strip_offset(block):
    return QB * block * (block + 1) // 2


def padded(rows, shards):
    unit = 16 * shards
    return (rows + unit - 1) // unit * unit


class Total:
    def __init__(self, NP, S, place, remote, buf, result, local, base, count, land_s, land_p, land_z, send, recv):
        self.NP, self.S = NP, S
        self.base, self.count = base, count
        self.result, self.local = result, local
        self.c, self.pr, self.z, self.own, self.other = place
        self.remote = remote
        self.buf, self.land_s, self.land_p, self.land_z = buf, land_s, land_p, land_z
        self.send, self.recv = send, recv
        self.part = count // NP
        self.shard = self.part // S

    def rows(self, pr, z=None):
        if z is None:
            return pl.ds(pl.multiple_of(self.base + pr * self.part, 16), self.part)
        return pl.ds(pl.multiple_of(self.base + pr * self.part + z * self.shard, 16), self.shard)

    def copy(self, src, dst, index, pr, z, c):
        return self.remote(src, dst, self.send.at[index], self.recv.at[index], 2 * pr + c, z)

    def core_scatter(self):
        return [self.copy(self.buf.at[pl.ds(self.base, self.count), self.other], self.land_s, 0, self.pr, self.z, 1 - self.c)]

    def core_gather(self):
        half = self.result.at[pl.ds(self.base, self.count), self.own]
        return [self.copy(half, half, 1, self.pr, self.z, 1 - self.c)]

    def pair_scatter(self):
        copies = []
        for k in range(1, self.NP):
            to = lax.rem(self.pr + k, self.NP)
            src = self.buf.at[self.rows(to), self.own]
            copies.append(self.copy(src, self.land_p.at[k - 1], 1 + k, to, self.z, self.c))
        return copies

    def pair_gather(self):
        copies = []
        for k in range(1, self.NP):
            to = lax.rem(self.pr + k, self.NP)
            src = self.result.at[self.rows(self.pr), self.own]
            copies.append(self.copy(src, src, self.NP + k, to, self.z, self.c))
        return copies

    def z_scatter(self):
        copies = []
        for k in range(1, self.S):
            to = lax.rem(self.z + k, self.S)
            src = self.buf.at[self.rows(self.pr, to), self.own]
            copies.append(self.copy(src, self.land_z.at[k - 1], 2 * self.NP - 1 + k, self.pr, to, self.c))
        return copies

    def z_gather(self):
        copies = []
        for k in range(1, self.S):
            to = lax.rem(self.z + k, self.S)
            rows = self.rows(self.pr, self.z)
            src, dst = self.buf.at[rows, self.own], self.result.at[rows, self.own]
            copies.append(self.copy(src, dst, 2 * self.NP + self.S - 2 + k, self.pr, to, self.c))
        return copies

    def keep(self):
        rows = self.rows(self.pr, self.z)
        return pltpu.make_async_copy(self.buf.at[rows, self.own], self.result.at[rows, self.own], self.local)

    @staticmethod
    def start(copies):
        for copy in copies:
            copy.start()

    @staticmethod
    def wait(copies):
        for copy in copies:
            copy.wait()

    def add(self, first, count, lands):
        size = self.shard

        @pl.loop(0, count)
        def _(i):
            rows = pl.ds(pl.multiple_of(self.base + first + i * size, 16), size)
            total = self.buf[rows, self.own].astype(f32)
            for land in lands:
                total = total + land[pl.ds(pl.multiple_of(i * size, 16), size), :].astype(f32)
            self.buf[rows, self.own] = total.astype(bf16)

    def core_add(self):
        self.wait(self.core_scatter())
        self.add(0, self.NP * self.S, [self.land_s])
        self.start(self.pair_scatter())

    def pair_add(self):
        self.wait(self.pair_scatter())
        self.add(self.pr * self.part, self.S, [self.land_p.at[k] for k in range(self.NP - 1)])
        self.start(self.z_scatter())

    def z_add(self):
        self.wait(self.z_scatter())
        self.add(self.pr * self.part + self.z * self.shard, 1, [self.land_z.at[k] for k in range(self.S - 1)])
        self.start([self.keep()] + self.z_gather())

    def z_done(self):
        self.wait([self.keep()] + self.z_gather())
        self.start(self.pair_gather())

    def pair_done(self):
        self.wait(self.pair_gather())
        self.start(self.core_gather())

    def core_done(self):
        self.wait(self.core_gather())


def fold_rows(values):
    rows, width = values.shape
    return jnp.sum(values.reshape(rows // 8, 8, width), axis=0)


def split_rows(rows, first, shards):
    unit = 16 * shards
    units = rows // unit
    head = first // unit
    mid = (units - head + 1) // 2
    return head * unit, mid * unit, (units - head - mid) * unit


def interleave(main, count_main, side, count_side):
    steps = max(count_main, count_side)
    done_main = done_side = 0
    for step in range(1, steps + 1):
        while done_main < step * count_main / steps:
            next(main, None)
            done_main += 1
        while done_side < step * count_side / steps:
            next(side, None)
            done_side += 1
    for _ in main:
        pass
    for _ in side:
        pass


def block_kernel(
    G, S, NP, T, L, D, FF,
    x, seg, cot, gain_a, gain_m, wq, wk, wv, wo, wgT, wuT, wd,
    out, gin, out_a, out_b,
    xs, cots, seg_other, first_s, cos_s, sin_s, n_s, wqkvT, gA, gB,
    qT, kT, vT, p_s, s_buf, inv_tot, mixT, mfull, nm, hid, dga, dup, da, dmT,
    dOT, dacc_k, dacc_v, g_ga, g_gm,
    land_s1, land_p1, land_z1, land_s2, land_p2, land_z2, land_s3, land_p3, land_z3, land_p4, land_z4,
    w_sem, loc_sem, seg_sem, x_send, x_recv, fwd_send, cot_send, cot_recv, mix_send, mix_recv,
    out_send, out_recv, dm_send, dm_recv, dn_send, dn_recv, gin_send, gin_recv, g_sem,
    t1_send, t1_recv, t2_send, t2_recv, t3_send, t3_recv, t4_send, t4_recv,
):
    d = lax.axis_index("dp")
    z = lax.axis_index("seq")
    c = lax.rem(d, 2)
    pair = d - c
    sib = pair + 1 - c
    gz = z // G
    lz = lax.rem(z, G)
    half = L // 2
    Dh = D // 2
    NH = Dh // HD

    def remote(src, dst, send, recv, dp, seq):
        return pltpu.make_async_remote_copy(
            src_ref=src, dst_ref=dst, send_sem=send, recv_sem=recv,
            device_id=(dp, seq), device_id_type=MESH,
        )

    own_cols = pl.ds(pl.multiple_of(c * Dh, Dh), Dh)
    other_cols = pl.ds(pl.multiple_of((1 - c) * Dh, Dh), Dh)
    pr = d // 2
    here_at = (c, pr, z, own_cols, other_cols)
    RA = gA.shape[0]
    count_1, count_2, count_3 = split_rows(RA, FF, NP * S)
    sum_1 = Total(
        NP, S, here_at, remote, gA, out_a, g_sem.at[0], 0, count_1, land_s1, land_p1, land_z1, t1_send, t1_recv
    )
    sum_2 = Total(
        NP, S, here_at, remote, gA, out_a, g_sem.at[1], count_1, count_2,
        land_s2, land_p2, land_z2, t2_send, t2_recv,
    )
    sum_3 = Total(
        NP, S, here_at, remote, gA, out_a, g_sem.at[2], count_1 + count_2, count_3,
        land_s3, land_p3, land_z3, t3_send, t3_recv,
    )
    sum_4 = Total(
        NP, S, here_at, remote, gB, out_b, g_sem.at[3], 0, gB.shape[0], None, land_p4, land_z4, t4_send, t4_recv
    )
    up_row, down_row, out_row, gain_row = FF, 2 * FF, 3 * FF, 3 * FF + D

    loads = [
        pltpu.make_async_copy(w.at[:, own_cols], gB.at[pl.ds(i * D, D), own_cols], w_sem.at[i])
        for i, w in enumerate((wq, wk, wv))
    ] + [
        pltpu.make_async_copy(wgT, gA.at[pl.ds(0, FF)], w_sem.at[3]),
        pltpu.make_async_copy(wuT, gA.at[pl.ds(up_row, FF)], w_sem.at[4]),
        pltpu.make_async_copy(wd, gA.at[pl.ds(down_row, FF)], w_sem.at[5]),
        pltpu.make_async_copy(wo, gA.at[pl.ds(out_row, D)], w_sem.at[6]),
    ]
    for load in loads:
        load.start()
    for buffer, used in ((gA, gain_row), (gB, 3 * D)):
        buffer[used:buffer.shape[0], :] = jnp.zeros((buffer.shape[0] - used, D), bf16)
    wo_s = gA.at[pl.ds(out_row, D)]

    barrier = pltpu.get_barrier_semaphore()
    for step in range(1, 2 * S):
        other = lax.rem(c * S + z + step, 2 * S)
        pl.semaphore_signal(
            barrier, inc=1, device_id=(pair + other // S, lax.rem(other, S)), device_id_type=MESH
        )
    for step in range(1, NP):
        pl.semaphore_signal(
            barrier, inc=1, device_id=(2 * lax.rem(pr + step, NP) + c, z), device_id_type=MESH
        )
    pl.semaphore_wait(barrier, 2 * S - 1 + NP - 1)

    seg_copy = remote(seg, seg_other, seg_sem.at[0], seg_sem.at[1], sib, z)
    seg_copy.start()

    def x_rows(index):
        return xs.at[pl.ds(pl.multiple_of(index * T, T), T)]

    def x_copy(l):
        return remote(x.at[l], x_rows(z), x_send.at[l], x_recv.at[z], d, c * G + l)

    own_x = pltpu.make_async_copy(x.at[lz], x_rows(z), loc_sem.at[0])
    own_fwd = remote(x.at[lz], x_rows(z), fwd_send.at[0], x_recv.at[z], sib, z)

    @pl.when(gz == c)
    def _():
        own_x.start()
        own_fwd.start()

    for l in range(G):
        @pl.when(c * G + l != z)
        def _():
            x_copy(l).start()

    for load in loads:
        load.wait()
    for i in range(3):
        wqkvT[i * Dh:(i + 1) * Dh, :] = gB[i * D:(i + 1) * D, own_cols].T
    seg_copy.wait()
    seg_mine = jnp.where(gz == c, seg[...], seg_other[...])
    row = jnp.zeros((1, L), jnp.int32)
    for l in range(G):
        row = jnp.where(lz == l, seg_mine[l:l + 1, :], row)
    ids = row.astype(f32)
    first = jnp.zeros((1, L), f32)
    for doc in range(1, DOCS):
        before = jnp.sum(jnp.where(ids < doc, 1.0, 0.0), axis=1, keepdims=True)
        first = jnp.where(ids >= doc, before, first)
    first_s[...] = jnp.broadcast_to(first, (8, L))
    token = lax.broadcasted_iota(jnp.int32, (1, L), 1).astype(f32)
    place = token - first
    order = lax.broadcasted_iota(jnp.int32, (HD // 2, 1), 0).astype(f32)
    frequency = jnp.exp(order * f32(-2.0 * 9.210340371976184 / HD))
    angle = place * frequency
    cos_s[...] = jnp.cos(angle)
    sin_s[...] = jnp.sin(angle)

    def rms(values):
        inverse = lax.rsqrt(jnp.mean(values * values, axis=-1, keepdims=True) + epsilon)
        return values * inverse, inverse

    def project(start, size):
        rows = pl.ds(start, size)
        plain, _ = rms(xs[rows, :].astype(f32))
        normed = (plain * gain_a[...]).astype(bf16)
        n_s[rows, :] = normed
        lin = dot(wqkvT[...], normed, 1, 1)
        cosine, sine = cos_s[:, rows], sin_s[:, rows]

        def rotated(base):
            parts = []
            for h in range(NH):
                a = lin[base + h * HD:base + h * HD + HD // 2]
                b = lin[base + h * HD + HD // 2:base + (h + 1) * HD]
                parts.append(jnp.concatenate([a * cosine - b * sine, b * cosine + a * sine], axis=0))
            return parts

        query = jnp.concatenate(rotated(0), axis=0).astype(bf16)
        qT[:, rows] = (query.astype(f32) * HD ** -0.5).astype(bf16)
        kT[:, rows] = jnp.concatenate(rotated(Dh), axis=0).astype(bf16)
        vT[:, rows] = lin[2 * Dh:].astype(bf16)

    for step in range(S):
        source = lax.rem(z + step, S)
        arrived = remote(x.at[0], x_rows(source), x_send.at[0], x_recv.at[source], sib, z)
        if step == 0:
            @pl.when(gz == c)
            def _():
                own_x.wait()

            @pl.when(gz != c)
            def _():
                arrived.wait_recv()
        else:
            arrived.wait_recv()

            @pl.when(gz == c)
            def _():
                remote(x_rows(source), x_rows(source), fwd_send.at[step], x_recv.at[source], sib, z).start()

        @pl.loop(0, T // QB)
        def _(i):
            project(pl.multiple_of(source * T + i * QB, QB), QB)

    for l in range(G):
        @pl.when(c * G + l != z)
        def _():
            x_copy(l).wait_send()

    @pl.when(gz == c)
    def _():
        own_fwd.wait_send()
        for step in range(1, S):
            remote(x.at[0], x_rows(z), fwd_send.at[step], x_recv.at[z], sib, z).wait_send()

    to_core = z // G
    slot = lax.rem(z, G)

    def cot_rows(index):
        return cots.at[pl.ds(pl.multiple_of(index * T, T), T)]

    def cot_copy(l):
        return remote(cot.at[l], cot_rows(slot), cot_send.at[l], cot_recv.at[slot], pair + to_core, c * G + l)

    own_cot = pltpu.make_async_copy(cot.at[lz], cot_rows(slot), loc_sem.at[1])
    keeps_own = (gz == c) & (to_core == c)
    for l in range(G):
        here = (c * G + l == z) & (to_core == c)

        @pl.when(jnp.logical_not(here))
        def _():
            cot_copy(l).start()

    @pl.when(keeps_own)
    def _():
        own_cot.start()

    NQ = L // QB

    def place_of(rows, first_row):
        return (lax.broadcasted_iota(jnp.int32, (rows, QB), 0) + first_row).astype(f32)

    def mask_of(tile, qb, kb):
        begin = first_s[0:1, qb * QB:(qb + 1) * QB]
        query_place = (lax.broadcasted_iota(jnp.int32, (1, QB), 1) + qb * QB).astype(f32)
        edge = qb in (0, NQ - 1)
        if edge:
            tile = jnp.where(place_of(QB, kb * QB) >= begin, tile, masked_value)
        elif kb == 0:
            head = jnp.where(place_of(EDGE, 0) >= begin, tile[:EDGE], masked_value)
            tile = jnp.concatenate([head, tile[EDGE:]], axis=0)
        if kb == qb:
            tile = jnp.where(place_of(QB, kb * QB) <= query_place, tile, masked_value)
        return tile

    def mix_copy(h):
        return remote(
            mixT.at[pl.ds(pl.multiple_of(h * HD, HD), HD), pl.ds(pl.multiple_of((1 - c) * half, half), half)],
            mfull.at[pl.ds(pl.multiple_of(c * Dh + h * HD, HD), HD), :],
            mix_send.at[h], mix_recv.at[h], sib, z,
        )

    order = [1] + list(range(NQ - 1, 1, -1)) + [0]

    @pl.loop(0, NH)
    def _(h):
        rows = pl.ds(pl.multiple_of(h * HD, HD), HD)
        tops = {}

        def score(turn):
            qb = order[turn]
            query = qT[rows, qb * QB:(qb + 1) * QB]
            top = None
            for kb in range(qb + 1):
                tile = mask_of(dot(kT[rows, kb * QB:(kb + 1) * QB], query, 0, 0), qb, kb)
                part = jnp.max(tile.reshape(QB // 8, 8, QB), axis=0)
                top = part if top is None else jnp.maximum(top, part)
                s_buf[turn % 2, kb * QB:(kb + 1) * QB, :] = tile
                yield
            tops[turn] = jnp.max(top, axis=0, keepdims=True)

        def weigh(turn):
            qb = order[turn]
            cols = slice(qb * QB, (qb + 1) * QB)
            depth, base = (qb + 1) * QB, strip_offset(qb)
            total = None
            for kb in range(qb + 1):
                expanded = jnp.exp(s_buf[turn % 2, kb * QB:(kb + 1) * QB, :] - tops[turn])
                part = jnp.sum(expanded.reshape(QB // 8, 8, QB), axis=0)
                total = part if total is None else total + part
                p_s[h, base + kb * QB:base + (kb + 1) * QB, :] = expanded.astype(bf16)
                yield
            inverse = 1.0 / jnp.sum(total, axis=0, keepdims=True)
            inv_tot[h, :, cols] = jnp.broadcast_to(inverse, (8, QB))
            low = p_s[h, base:base + depth, :]
            mixT[rows, cols] = (dot(vT[rows, 0:depth], low, 1, 0) * inverse).astype(bf16)

        for _ in score(0):
            pass
        for turn, qb in enumerate(order):
            more = turn + 1 < len(order)
            interleave(
                score(turn + 1) if more else iter(()), order[turn + 1] + 1 if more else 0, weigh(turn), qb + 1
            )
        mix_copy(h).start()
        mfull[pl.ds(pl.multiple_of(c * Dh + h * HD, HD), HD), :] = mixT[
            rows, pl.ds(pl.multiple_of(c * half, half), half)
        ]

    @pl.loop(0, NH)
    def _(h):
        mix_copy(h).wait_send()
        remote(
            mixT.at[0:HD, 0:half], mfull.at[pl.ds(pl.multiple_of((1 - c) * Dh + h * HD, HD), HD), :],
            mix_send.at[h], mix_recv.at[h], sib, z,
        ).wait_recv()

    own_rows = pl.ds(pl.multiple_of(c * Dh, Dh), Dh)

    ff_cuts = [(first_col, min(first_col + 512, FF)) for first_col in range(0, FF, 512)]
    g_gm[...] = jnp.zeros((8, D), f32)
    NB = half // MB
    per = T // MB

    def back_copy(i, src, row, dst, send, recv):
        inside = pl.ds(pl.multiple_of(lax.rem(i, per) * MB, MB), MB)
        return remote(
            src.at[pl.ds(pl.multiple_of(row, MB), MB)], dst.at[lz, inside],
            send.at[i], recv.at[lz * per + lax.rem(i, per)], pair + gz, c * G + i // per,
        )

    def back_local(i, src, row, dst, local):
        inside = pl.ds(pl.multiple_of(lax.rem(i, per) * MB, MB), MB)
        return pltpu.make_async_copy(src.at[pl.ds(pl.multiple_of(row, MB), MB)], dst.at[lz, inside], local.at[lax.rem(i, per)])

    def stays(i):
        return (gz == c) & (c * G + i // per == z)

    def back_start(i, src, row, dst, send, recv, local):
        @pl.when(jnp.logical_not(stays(i)))
        def _():
            back_copy(i, src, row, dst, send, recv).start()

        @pl.when(stays(i))
        def _():
            back_local(i, src, row, dst, local).start()

    def back_wait(src, row, dst, send, recv, local):
        @pl.loop(0, NB)
        def _(i):
            @pl.when(jnp.logical_not(stays(i)))
            def _():
                back_copy(i, src, row + i * MB, dst, send, recv).wait_send()

            @pl.when(stays(i))
            def _():
                back_local(i, src, row + i * MB, dst, local).wait()
        for l in range(G):
            mine = (c * G + l == z) & (gz == c)
            for part in range(per):
                @pl.when(jnp.logical_not(mine))
                def _():
                    remote(
                        src.at[pl.ds(0, MB)], dst.at[l, pl.ds(part * MB, MB)],
                        send.at[0], recv.at[l * per + part], sib, z,
                    ).wait_recv()

    @pl.loop(0, NB)
    def _(i):
        start = pl.multiple_of(i * MB, MB)
        rows = pl.ds(start, MB)
        mine = stays(i)

        @pl.when((lax.rem(i, per) == 0) & jnp.logical_not(mine))
        def _():
            remote(cot.at[0], cot_rows(i // per), cot_send.at[0], cot_recv.at[i // per], sib, z).wait_recv()

        @pl.when((lax.rem(i, per) == 0) & mine)
        def _():
            own_cot.wait()

        base = xs[pl.ds(pl.multiple_of(c * half + start, MB), MB), :].astype(f32)
        middle = base + dot(mfull[:, rows], wo_s[...], 0, 0)
        plain, inverse = rms(middle)
        gain = gain_m[...]
        normed = (plain * gain).astype(bf16)
        nm[rows, :] = normed
        grad = cots[rows, :]
        result = middle
        d_normed = None
        for first_col, last_col in ff_cuts:
            cut = slice(first_col, last_col)
            cut_up = slice(up_row + first_col, up_row + last_col)
            cut_down = slice(down_row + first_col, down_row + last_col)
            gate = dot(normed, gA[cut, :], 1, 1)
            up = dot(normed, gA[cut_up, :], 1, 1)
            sig = 1.0 / (1.0 + jnp.exp(-gate))
            act = gate * sig
            hidden = (act * up).astype(bf16)
            hid[rows, cut] = hidden
            result = result + dot(hidden, gA[cut_down, :], 1, 0)
            d_hidden = dot(grad, gA[cut_down, :], 1, 1)
            d_gate = (d_hidden * up * sig * (1.0 + gate * (1.0 - sig))).astype(bf16)
            d_up = (d_hidden * act).astype(bf16)
            dga[rows, cut] = d_gate
            dup[rows, cut] = d_up
            term = dot(d_gate, gA[cut, :], 1, 0) + dot(d_up, gA[cut_up, :], 1, 0)
            d_normed = term if d_normed is None else d_normed + term
        spare = pl.multiple_of((1 - c) * half + start, MB)
        xs[pl.ds(spare, MB), :] = result.astype(bf16)
        back_start(i, xs, spare, out, out_send, out_recv, loc_sem.at[pl.ds(2, per)])
        scaled = d_normed * gain
        g_gm[...] += fold_rows(d_normed * plain)
        d_middle = grad.astype(f32) + inverse * (scaled - plain * jnp.mean(scaled * plain, axis=-1, keepdims=True))
        d_attn = d_middle.astype(bf16)
        da[rows, :] = d_attn
        dmT[:, rows] = dot(wo_s[...], d_attn, 1, 1).astype(bf16)

    dm_copy = remote(
        dmT.at[pl.ds(pl.multiple_of((1 - c) * Dh, Dh), Dh), :],
        dOT.at[:, pl.ds(pl.multiple_of(c * half, half), half)], dm_send.at[0], dm_recv.at[0], sib, z
    )
    dm_copy.start()

    for l in range(G):
        here = (c * G + l == z) & (to_core == c)

        @pl.when(jnp.logical_not(here))
        def _():
            cot_copy(l).wait_send()

    def ff_grad(target, base, left, right):
        for first_row in range(0, FF, 512):
            last_row = min(first_row + 512, FF)
            grad = dot(left[:, first_row:last_row], right[...], 0, 0)
            target[base + first_row:base + last_row, :] = grad.astype(bf16)

    ff_grad(gA, 0, dga, nm)
    sum_1.start(sum_1.core_scatter())
    ff_grad(gA, up_row, dup, nm)
    ff_grad(gA, down_row, hid, cots)
    sum_2.start(sum_2.core_scatter())
    gA[out_row:out_row + D, :] = dot(mfull[...], da[...], 1, 0).astype(bf16)
    gA[gain_row:gain_row + 16, :] = jnp.concatenate([g_gm[...], jnp.zeros((8, D), f32)], axis=0).astype(bf16)
    sum_3.start(sum_3.core_scatter())
    sum_1.core_add()

    dm_copy.wait()
    dOT[:, pl.ds(pl.multiple_of(c * half, half), half)] = dmT[own_rows, :]
    sum_2.core_add()
    sum_3.core_add()

    parts = (dga, dup, hid)

    def unrotated(values, cosine, sine):
        a, b = values[:HD // 2], values[HD // 2:]
        return jnp.concatenate([a * cosine + b * sine, b * cosine - a * sine], axis=0)

    @pl.loop(0, NH)
    def _(h):
        rows = pl.ds(pl.multiple_of(h * HD, HD), HD)

        def score_back(qb):
            cols = slice(qb * QB, (qb + 1) * QB)
            depth, base = (qb + 1) * QB, strip_offset(qb)
            grad_wide = dOT[rows, cols].astype(f32) * inv_tot[h, 0:1, cols]
            delta = jnp.sum(grad_wide * mixT[rows, cols].astype(f32), axis=0, keepdims=True)
            grad = grad_wide.astype(bf16)
            add_v = dot(grad, p_s[h, base:base + depth, :], 1, 1)
            if qb == NQ - 1:
                dacc_v[:, 0:depth] = add_v
            else:
                dacc_v[:, 0:depth] += add_v
            yield
            for kb in range(qb + 1):
                tile = slice(base + kb * QB, base + (kb + 1) * QB)
                d_probs = dot(vT[rows, kb * QB:(kb + 1) * QB], grad, 0, 0)
                p_s[h, tile, :] = (p_s[h, tile, :].astype(f32) * (d_probs - delta)).astype(bf16)
                yield

        def spread_back(qb):
            cols = slice(qb * QB, (qb + 1) * QB)
            depth, base = (qb + 1) * QB, strip_offset(qb)
            d_scores = p_s[h, base:base + depth, :]
            add_k = dot(qT[rows, cols], d_scores, 1, 1)
            if qb == NQ - 1:
                dacc_k[:, 0:depth] = add_k
            else:
                dacc_k[:, 0:depth] += add_k
            yield
            d_query = dot(kT[rows, 0:depth], d_scores, 1, 0) * HD ** -0.5
            side, lane = divmod(qb * QB, half)
            parts[0][pl.ds(pl.multiple_of(side * Dh + h * HD, HD), HD), lane:lane + QB] = unrotated(
                d_query.astype(bf16).astype(f32), cos_s[:, cols], sin_s[:, cols]
            ).astype(bf16)
            yield

        for _ in score_back(NQ - 1):
            pass
        for qb in reversed(range(NQ)):
            interleave(score_back(qb - 1) if qb else iter(()), qb + 1 if qb else 0, spread_back(qb), 2)
        for side in range(2):
            cols = slice(side * half, (side + 1) * half)
            place_rows = pl.ds(pl.multiple_of(side * Dh + h * HD, HD), HD)
            parts[1][place_rows, 0:half] = unrotated(
                dacc_k[:, cols].astype(bf16).astype(f32), cos_s[:, cols], sin_s[:, cols]
            ).astype(bf16)
            parts[2][place_rows, 0:half] = dacc_v[:, cols].astype(bf16)
        pl.when(h == 1)(sum_1.pair_add)

    sum_2.pair_add()
    sum_1.z_add()

    def back_norm(side, start):
        side_rows = pl.ds(pl.multiple_of(side * Dh, Dh), Dh)
        total = None
        for i in range(3):
            term = dot(parts[i][side_rows, pl.ds(start, MB)], wqkvT[i * Dh:(i + 1) * Dh, :], 0, 0)
            total = term if total is None else total + term
        return total

    @pl.loop(0, half // MB)
    def _(i):
        start = pl.multiple_of(i * MB, MB)
        nm[pl.ds(start, MB), :] = back_norm(1 - c, start).astype(bf16)

    dn_in = cots
    dn_copy = remote(nm, dn_in, dn_send.at[0], dn_recv.at[0], sib, z)
    dn_copy.start()

    for i in range(3):
        grad = dot(parts[i][0:Dh, 0:half], n_s[0:half, :], 1, 0)
        grad = grad + dot(parts[i][Dh:2 * Dh, 0:half], n_s[half:L, :], 1, 0)
        gB[i * D:(i + 1) * D, own_cols] = grad.T.astype(bf16)
    back_wait(xs, (1 - c) * half, out, out_send, out_recv, loc_sem.at[pl.ds(2, per)])
    dn_copy.wait()

    g_ga[...] = jnp.zeros((8, D), f32)

    @pl.loop(0, NB)
    def _(i):
        start = pl.multiple_of(i * MB, MB)
        rows = pl.ds(start, MB)
        own = pl.ds(pl.multiple_of(c * half + start, MB), MB)
        d_normed = back_norm(c, start) + dn_in[rows, :].astype(f32)
        plain, inverse = rms(xs[own, :].astype(f32))
        scaled = d_normed * gain_a[...]
        g_ga[...] += fold_rows(d_normed * plain)
        d_start = inverse * (scaled - plain * jnp.mean(scaled * plain, axis=-1, keepdims=True))
        nm[rows, :] = (da[rows, :].astype(f32) + d_start).astype(bf16)
        back_start(i, nm, start, gin, gin_send, gin_recv, loc_sem.at[pl.ds(2 + per, per)])

    gB[3 * D:3 * D + 16, own_cols] = jnp.concatenate([g_ga[:, :Dh], g_ga[:, Dh:]], axis=0).astype(bf16)
    sum_4.start(sum_4.pair_scatter())
    sum_1.z_done()
    sum_3.pair_add()
    sum_2.z_add()
    sum_1.pair_done()
    sum_2.z_done()
    sum_3.z_add()
    sum_4.pair_add()
    sum_3.z_done()
    sum_1.core_done()
    sum_2.pair_done()
    sum_4.z_add()
    sum_3.pair_done()
    sum_4.z_done()
    sum_2.core_done()
    sum_4.pair_done()
    sum_3.core_done()
    back_wait(nm, 0, gin, gin_send, gin_recv, loc_sem.at[pl.ds(2 + per, per)])
    sum_4.core_done()


def on_device(
    G, S, NP,
    inputs, segment_ids, cotangent, norm_attn, norm_mlp, w_query, w_key, w_value, w_out, w_gate, w_up, w_down,
):
    _, T, D = inputs.shape
    FF = w_gate.shape[1]
    L = T * S
    half, Dh = L // 2, D // 2
    NH = Dh // HD
    anywhere = pl.BlockSpec(memory_space=pl.ANY)
    vmem = pl.BlockSpec(memory_space=pltpu.VMEM)
    dma = pltpu.SemaphoreType.DMA

    def buf(*shape, dtype=bf16):
        return pltpu.VMEM(shape, dtype)

    strips = strip_offset(L // QB)
    shards = NP * S
    RA, RB = padded(3 * FF + D + 16, shards), padded(3 * D + 16, shards)

    def lands(rows, core):
        kept = [buf(rows, Dh)] if core else []
        return kept + [buf(NP - 1, rows // NP, Dh), buf(S - 1, rows // shards, Dh)]

    steps = 2 + 2 * (NP - 1) + 2 * (S - 1)
    NB, per = half // MB, T // MB
    out, gin, out_a, out_b = pl.pallas_call(
        functools.partial(block_kernel, G, S, NP, T, L, D, FF),
        out_shape=[
            jax.ShapeDtypeStruct((G, T, D), bf16),
            jax.ShapeDtypeStruct((G, T, D), bf16),
            jax.ShapeDtypeStruct((RA, D), bf16),
            jax.ShapeDtypeStruct((RB, D), bf16),
        ],
        in_specs=[anywhere, vmem, anywhere, vmem, vmem] + [anywhere] * 7,
        out_specs=[anywhere] * 4,
        scratch_shapes=[
            buf(L, D), buf(half, D), buf(G, L, dtype=jnp.int32), buf(8, L, dtype=f32),
            buf(HD // 2, L, dtype=f32), buf(HD // 2, L, dtype=f32),
            buf(L, D), buf(3 * Dh, D), buf(RA, D), buf(RB, D),
            buf(Dh, L), buf(Dh, L), buf(Dh, L),
            buf(NH, strips, QB), buf(2, L, QB, dtype=f32), buf(NH, 8, L, dtype=f32), buf(Dh, L), buf(D, half),
            buf(half, D), buf(half, FF), buf(half, FF), buf(half, FF),
            buf(half, D), buf(D, half),
            buf(Dh, L), buf(HD, L, dtype=f32), buf(HD, L, dtype=f32),
            buf(8, D, dtype=f32), buf(8, D, dtype=f32),
            *(land for rows in split_rows(RA, FF, shards) for land in lands(rows, True)), *lands(RB, False),
            dma((7,)), dma((2 + 2 * per,)), dma((2,)), dma((G,)), dma((S,)), dma((S,)), dma((G,)), dma((G,)),
            dma((NH,)), dma((NH,)), dma((NB,)), dma((G * per,)), dma((1,)), dma((1,)), dma((1,)), dma((1,)),
            dma((NB,)), dma((G * per,)), dma((4,)),
            *([dma((steps,))] * 8),
        ],
        compiler_params=pltpu.CompilerParams(
            collective_id=0, has_side_effects=True, vmem_limit_bytes=63 * 2**20
        ),
    )(
        inputs, segment_ids, cotangent, norm_attn.reshape(1, D), norm_mlp.reshape(1, D),
        w_query, w_key, w_value, w_out, w_gate.T, w_up.T, w_down,
    )

    last_a, last_b = 3 * FF + D, 3 * D
    gain_attn = jnp.sum(out_b[last_b:last_b + 16].astype(f32).reshape(2, 8, 2, Dh), axis=(1, 2)).reshape(D)
    gain_mlp = jnp.sum(out_a[last_a:last_a + 8].astype(f32), axis=0)
    return (
        out, gin.astype(f32), gain_attn, gain_mlp,
        out_b[:D].astype(f32), out_b[D:2 * D].astype(f32), out_b[2 * D:3 * D].astype(f32),
        out_a[3 * FF:last_a].astype(f32), out_a[:FF].astype(f32).T, out_a[FF:2 * FF].astype(f32).T,
        out_a[2 * FF:3 * FF].astype(f32),
    )


def solution(mesh):
    S = mesh.shape["seq"]
    NP = mesh.shape["dp"] // 2
    rows = P("dp", "seq", None)
    return jax.shard_map(
        functools.partial(on_device, S // 2, S, NP),
        mesh=mesh,
        in_specs=(rows, P("dp", None), rows) + (P(),) * 9,
        out_specs=(rows, rows) + (P(),) * 9,
        check_vma=False,
    )
```

time: 353 us -> 193 us (0.55)
  blocking collectives: 192 us -> 0 us
  Pallas kernels: 124 us -> 177 us
  local copies, waits for them, and re-layouts: 18.8 us -> 2.28 us
  between operations: 14.2 us -> 0.67 us
  other arithmetic: 2.83 us -> 11.5 us
    psum x1 -> x0, blocking collectives: 192 us -> none  [on_device(): return (out, gin.astype(f32)) + tuple(lax.psum(grads, ('dp', 'seq')))]
    pallas_call x1, Pallas kernels: 124 us -> 177 us  [on_device(): pl.pallas_call(functools.partial(block_kernel, G, S, NP, T, L, D, FF), ou...]
    unnamed x30 -> x8, local copies, waits for them, and re-layouts: 18.4 us -> 1.56 us
    convert_element_type x1 -> x3, other arithmetic: 1.61 us -> 10.1 us  [the longest x1 3.81 us: on_device(): out_a[2 * FF:3 * FF].astype(f32)]
  transfers between devices with their start and end apart: 1 -> 0, of which waited for: 0 -> 0; matrix products, arithmetic and copies ran while one was open for 2% -> 0% of each run, Pallas kernels for 0% -> 0%
where the time goes in v2:
time: 193 us; the launch traced here: 191 us
  Pallas kernels  177 us (92%)
  other arithmetic  11.5 us (6%)
  local copies, waits for them, and re-layouts  2.28 us (1%)
    pallas_call x1, Pallas kernels, on_device(): pl.pallas_call(functools.partial(block_kernel, G, S, NP, T, L, D, FF), ou...  177 us

profile of v2, /device:TPU:0, one launch (start us, length us, event | category | flops | bytes accessed | tf_op | source)
XLA Modules:
  0.0 191.1 jit_solution(699399063814127634)
XLA Ops:
  0.6 176.7 %shard_map.203 = (bf16[2,512,512]{2,1,0:T(8,128)(2,1)}, bf16[2,512,512]{2,1,0:T(8,128)(2,1)}, bf16[4864,512]{1,0:T(8,128)(2,1)}, bf16[1792,512]{1,0:T(8,128)(2,1)}) custom-call(bf16[2,512,512]{2,1,0:T(8,128)(2,1)} %x.1, s32[2,2048]{1,0:T(2,128)} %seg.1, bf16[2,512,512]{2,1,0:T(8,128)(2,1)} %cot.1, f32[1,512]{1,0:T(1,128)} %bitcast.17, f32[1,512]{1,0:T(1,128)} %bitcast.18, ...), custom_call_target="tpu_custom_call" | custom-call | tf_op jit(solution)/shard_map/pallas_call | solution.py:745
  177.3 0.0 copy-start.1
  177.3 1.4 convert_reduce_fusion.1
  178.8 0.7 slice.27
  179.5 0.6 copy.23
  180.1 2.8 %convert_element_type.24 = f32[2,512,512]{2,1,0:T(8,128)} convert(bf16[2,512,512]{2,1,0:T(8,128)(2,1)} %get-tuple-element.16) | non-fusion elementwise | flops 524288 | bytes 3145728 | tf_op jit(solution)/shard_map/convert_element_type | solution.py:783
  182.9 0.0 copy-done.1
  182.9 0.0 copy-start
  182.9 3.4 %slice_convert_fusion.2 = (f32[512,512]{1,0:T(8,128)}, f32[512,512]{1,0:T(8,128)}, f32[512,512]{1,0:T(8,128)}, f32[512,512]{1,0:T(8,128)}) fusion(bf16[1792,512]{1,0:T(8,128)(2,1)S(1)} %copy-done.1, bf16[4864,512]{1,0:T(8,128)(2,1)} %get-tuple-element.18), kind=kLoop, calls=%fused_computation.4 | loop fusion | flops 1048576 | bytes 6291456 | tf_op jit(solution)/shard_map/convert_element_type | solution.py:784
  186.3 0.0 copy-done
  186.3 0.0 copy-start.2
  186.4 3.8 %slice_convert_fusion = (f32[1376,512]{1,0:T(8,128)}, f32[512,1376]{0,1:T(8,128)}, f32[512,1376]{0,1:T(8,128)}) fusion(bf16[4864,512]{1,0:T(8,128)(2,1)S(1)} %copy-done), kind=kLoop, calls=%fused_computation.2 | loop fusion | flops 2113536 | bytes 12681216 | tf_op jit(solution)/shard_map/convert_element_type | solution.py:786
  190.2 0.0 copy-done.2
  190.2 1.0 copy.25
  (1 shorter events, 0.0 us)
Async XLA Ops:
  177.3 5.6 %copy-start.1 = (bf16[1792,512]{1,0:T(8,128)(2,1)S(1)}, bf16[1792,512]{1,0:T(8,128)(2,1)}, u32[]{:S(2)}) copy-start(bf16[1792,512]{1,0:T(8,128)(2,1)} %get-tuple-element.17) | copy-start | bytes 5505028
  182.9 3.4 %copy-start = (bf16[4864,512]{1,0:T(8,128)(2,1)S(1)}, bf16[4864,512]{1,0:T(8,128)(2,1)}, u32[]{:S(2)}) copy-start(bf16[4864,512]{1,0:T(8,128)(2,1)} %get-tuple-element.18) | copy-start | bytes 14942212
  186.3 3.8 %copy-start.2 = (bf16[2,512,512]{2,1,0:T(8,128)(2,1)S(1)}, bf16[2,512,512]{2,1,0:T(8,128)(2,1)}, u32[]{:S(2)}) copy-start(bf16[2,512,512]{2,1,0:T(8,128)(2,1)} %get-tuple-element.37) | copy-start | bytes 3145732

commit v3 on v2

--- a/solution.py
+++ b/solution.py
@@ -17,6 +17,10 @@
 bf16 = jnp.bfloat16
 QB = 256
 MB = 256
+SCHEDULE = (
+    4, 3, 1, 0, 2, 5, 3, 1, 2, 4, 6, 3, 5, 4, 2, 0, 1, 7, 3, 2, 8, 5,
+    0, 9, 0, 1, 1, 2, 3, 2, 3, 5, 5,
+)
 EDGE = 128
 
 
@@ -35,116 +39,102 @@
     return (rows + unit - 1) // unit * unit
 
 
+class Axis:
+    def __init__(self, size, index, device):
+        self.size, self.index, self.device = size, index, device
+
+    def others(self):
+        return [lax.rem(self.index + k, self.size) for k in range(1, self.size)]
+
+
+def lands(rows, sizes, core, width):
+    shapes = [(rows, width)] if core else []
+    for size in sizes:
+        rows //= size
+        shapes.append((size - 1, rows, width))
+    return shapes
+
+
+def copies_of(sizes):
+    return 2 + 2 * sum(size - 1 for size in sizes)
+
+
 class Total:
-    def __init__(self, NP, S, place, remote, buf, result, local, base, count, land_s, land_p, land_z, send, recv):
-        self.NP, self.S = NP, S
+    def __init__(self, remote, core, axes, own, other, buf, result, local, base, count, land, send, recv):
+        self.remote, self.core, self.axes, self.own, self.other = remote, core, axes, own, other
+        self.buf, self.result, self.local = buf, result, local
         self.base, self.count = base, count
-        self.result, self.local = result, local
-        self.c, self.pr, self.z, self.own, self.other = place
-        self.remote = remote
-        self.buf, self.land_s, self.land_p, self.land_z = buf, land_s, land_p, land_z
         self.send, self.recv = send, recv
-        self.part = count // NP
-        self.shard = self.part // S
-
-    def rows(self, pr, z=None):
-        if z is None:
-            return pl.ds(pl.multiple_of(self.base + pr * self.part, 16), self.part)
-        return pl.ds(pl.multiple_of(self.base + pr * self.part + z * self.shard, 16), self.shard)
-
-    def copy(self, src, dst, index, pr, z, c):
-        return self.remote(src, dst, self.send.at[index], self.recv.at[index], 2 * pr + c, z)
-
-    def core_scatter(self):
-        return [self.copy(self.buf.at[pl.ds(self.base, self.count), self.other], self.land_s, 0, self.pr, self.z, 1 - self.c)]
-
-    def core_gather(self):
-        half = self.result.at[pl.ds(self.base, self.count), self.own]
-        return [self.copy(half, half, 1, self.pr, self.z, 1 - self.c)]
-
-    def pair_scatter(self):
-        copies = []
-        for k in range(1, self.NP):
-            to = lax.rem(self.pr + k, self.NP)
-            src = self.buf.at[self.rows(to), self.own]
-            copies.append(self.copy(src, self.land_p.at[k - 1], 1 + k, to, self.z, self.c))
-        return copies
-
-    def pair_gather(self):
-        copies = []
-        for k in range(1, self.NP):
-            to = lax.rem(self.pr + k, self.NP)
-            src = self.result.at[self.rows(self.pr), self.own]
-            copies.append(self.copy(src, src, self.NP + k, to, self.z, self.c))
-        return copies
-
-    def z_scatter(self):
-        copies = []
-        for k in range(1, self.S):
-            to = lax.rem(self.z + k, self.S)
-            src = self.buf.at[self.rows(self.pr, to), self.own]
-            copies.append(self.copy(src, self.land_z.at[k - 1], 2 * self.NP - 1 + k, self.pr, to, self.c))
-        return copies
-
-    def z_gather(self):
-        copies = []
-        for k in range(1, self.S):
-            to = lax.rem(self.z + k, self.S)
-            rows = self.rows(self.pr, self.z)
-            src, dst = self.buf.at[rows, self.own], self.result.at[rows, self.own]
-            copies.append(self.copy(src, dst, 2 * self.NP + self.S - 2 + k, self.pr, to, self.c))
-        return copies
-
-    def keep(self):
-        rows = self.rows(self.pr, self.z)
-        return pltpu.make_async_copy(self.buf.at[rows, self.own], self.result.at[rows, self.own], self.local)
-
-    @staticmethod
-    def start(copies):
-        for copy in copies:
+        sizes = [axis.size for axis in axes]
+        self.with_core = len(land) > len(sizes)
+        self.land = list(land)
+        self.starts, self.counts, self.first_sem = [base], [count], [2]
+        for axis in axes:
+            self.counts.append(self.counts[-1] // axis.size)
+            self.starts.append(self.starts[-1] + axis.index * self.counts[-1])
+            self.first_sem.append(self.first_sem[-1] + 2 * (axis.size - 1))
+        self.stages = [("core", 0)] if self.with_core else []
+        self.stages += [("scatter", k) for k in range(len(axes))]
+        self.stages += [("gather", k) for k in reversed(range(len(axes)))]
+        self.stages.append(("back", 0))
+        self.at = 0
+
+    def rows(self, start, count):
+        return pl.ds(pl.multiple_of(start, 16), count)
+
+    def copies(self, stage):
+        kind, k = stage
+        if kind == "core":
+            src = self.buf.at[pl.ds(self.base, self.count), self.other]
+            return [self.remote(src, self.land[0], self.send.at[0], self.recv.at[0], *self.core)]
+        if kind == "back":
+            half = self.result.at[pl.ds(self.base, self.count), self.own]
+            return [self.remote(half, half, self.send.at[1], self.recv.at[1], *self.core)]
+        axis, count = self.axes[k], self.counts[k + 1]
+        land = self.land[k + self.with_core]
+        made = []
+        for slot, to in enumerate(axis.others()):
+            if kind == "scatter":
+                src = self.buf.at[self.rows(self.starts[k] + to * count, count), self.own]
+                dst, sem = land.at[slot], self.first_sem[k] + slot
+            else:
+                rows = self.rows(self.starts[k + 1], count)
+                source = self.buf if k == len(self.axes) - 1 else self.result
+                src, dst = source.at[rows, self.own], self.result.at[rows, self.own]
+                sem = self.first_sem[k] + axis.size - 1 + slot
+            made.append(self.remote(src, dst, self.send.at[sem], self.recv.at[sem], *axis.device(to)))
+        if kind == "gather" and k == len(self.axes) - 1:
+            rows = self.rows(self.starts[k + 1], count)
+            made.append(pltpu.make_async_copy(self.buf.at[rows, self.own], self.result.at[rows, self.own], self.local))
+        return made
+
+    def add(self, start, count, land):
+        chunk = self.counts[-1]
+
+        @pl.loop(0, count // chunk)
+        def _(i):
+            rows = self.rows(start + i * chunk, chunk)
+            total = self.buf[rows, self.own].astype(f32)
+            for piece in land:
+                total = total + piece[self.rows(i * chunk, chunk), :].astype(f32)
+            self.buf[rows, self.own] = total.astype(bf16)
+
+    def begin(self):
+        for copy in self.copies(self.stages[self.at]):
             copy.start()
 
-    @staticmethod
-    def wait(copies):
-        for copy in copies:
+    def advance(self):
+        kind, k = stage = self.stages[self.at]
+        for copy in self.copies(stage):
             copy.wait()
-
-    def add(self, first, count, lands):
-        size = self.shard
-
-        @pl.loop(0, count)
-        def _(i):
-            rows = pl.ds(pl.multiple_of(self.base + first + i * size, 16), size)
-            total = self.buf[rows, self.own].astype(f32)
-            for land in lands:
-                total = total + land[pl.ds(pl.multiple_of(i * size, 16), size), :].astype(f32)
-            self.buf[rows, self.own] = total.astype(bf16)
-
-    def core_add(self):
-        self.wait(self.core_scatter())
-        self.add(0, self.NP * self.S, [self.land_s])
-        self.start(self.pair_scatter())
-
-    def pair_add(self):
-        self.wait(self.pair_scatter())
-        self.add(self.pr * self.part, self.S, [self.land_p.at[k] for k in range(self.NP - 1)])
-        self.start(self.z_scatter())
-
-    def z_add(self):
-        self.wait(self.z_scatter())
-        self.add(self.pr * self.part + self.z * self.shard, 1, [self.land_z.at[k] for k in range(self.S - 1)])
-        self.start([self.keep()] + self.z_gather())
-
-    def z_done(self):
-        self.wait([self.keep()] + self.z_gather())
-        self.start(self.pair_gather())
-
-    def pair_done(self):
-        self.wait(self.pair_gather())
-        self.start(self.core_gather())
-
-    def core_done(self):
-        self.wait(self.core_gather())
+        if kind == "core":
+            self.add(self.base, self.count, [self.land[0]])
+        elif kind == "scatter":
+            land = self.land[k + self.with_core]
+            self.add(self.starts[k + 1], self.counts[k + 1], [land.at[slot] for slot in range(self.axes[k].size - 1)])
+        self.at += 1
+        if self.at < len(self.stages):
+            self.begin()
 
 
 def fold_rows(values):
@@ -152,12 +142,16 @@
     return jnp.sum(values.reshape(rows // 8, 8, width), axis=0)
 
 
-def split_rows(rows, first, shards):
+def split_rows(rows, first, second, shards):
     unit = 16 * shards
-    units = rows // unit
-    head = first // unit
-    mid = (units - head + 1) // 2
-    return head * unit, mid * unit, (units - head - mid) * unit
+    edges = [0, first // unit * unit, second // unit * unit]
+    edges += [(edges[2] + rows + unit) // 2 // unit * unit, rows]
+    return [(start, end - start) for start, end in zip(edges, edges[1:])]
+
+
+def axis_sizes(NP, S):
+    fast = 2 if NP % 2 == 0 else 1
+    return [fast, NP // fast, 2, S // 2], [NP // fast, fast, 2, S // 2], [NP, S]
 
 
 def interleave(main, count_main, side, count_side):
@@ -183,10 +177,9 @@
     xs, cots, seg_other, first_s, cos_s, sin_s, n_s, wqkvT, gA, gB,
     qT, kT, vT, p_s, s_buf, inv_tot, mixT, mfull, nm, hid, dga, dup, da, dmT,
     dOT, dacc_k, dacc_v, g_ga, g_gm,
-    land_s1, land_p1, land_z1, land_s2, land_p2, land_z2, land_s3, land_p3, land_z3, land_p4, land_z4,
     w_sem, loc_sem, seg_sem, x_send, x_recv, fwd_send, cot_send, cot_recv, mix_send, mix_recv,
     out_send, out_recv, dm_send, dm_recv, dn_send, dn_recv, gin_send, gin_recv, g_sem,
-    t1_send, t1_recv, t2_send, t2_recv, t3_send, t3_recv, t4_send, t4_recv,
+    *rest,
 ):
     d = lax.axis_index("dp")
     z = lax.axis_index("seq")
@@ -208,23 +201,45 @@
     own_cols = pl.ds(pl.multiple_of(c * Dh, Dh), Dh)
     other_cols = pl.ds(pl.multiple_of((1 - c) * Dh, Dh), Dh)
     pr = d // 2
-    here_at = (c, pr, z, own_cols, other_cols)
-    RA = gA.shape[0]
-    count_1, count_2, count_3 = split_rows(RA, FF, NP * S)
-    sum_1 = Total(
-        NP, S, here_at, remote, gA, out_a, g_sem.at[0], 0, count_1, land_s1, land_p1, land_z1, t1_send, t1_recv
-    )
-    sum_2 = Total(
-        NP, S, here_at, remote, gA, out_a, g_sem.at[1], count_1, count_2,
-        land_s2, land_p2, land_z2, t2_send, t2_recv,
-    )
-    sum_3 = Total(
-        NP, S, here_at, remote, gA, out_a, g_sem.at[2], count_1 + count_2, count_3,
-        land_s3, land_p3, land_z3, t3_send, t3_recv,
-    )
-    sum_4 = Total(
-        NP, S, here_at, remote, gB, out_b, g_sem.at[3], 0, gB.shape[0], None, land_p4, land_z4, t4_send, t4_recv
-    )
+    fast = 2 if NP % 2 == 0 else 1
+    row_at, col_at = pr // fast, lax.rem(pr, fast)
+    low, high = lax.rem(z, 2), z // 2
+    axis_x = Axis(fast, col_at, lambda j: (2 * (row_at * fast + j) + c, z))
+    axis_y = Axis(NP // fast, row_at, lambda j: (2 * (j * fast + col_at) + c, z))
+    axis_near = Axis(2, low, lambda j: (d, high * 2 + j))
+    axis_far = Axis(S // 2, high, lambda j: (d, j * 2 + low))
+    rest = list(rest)
+
+    def take(count):
+        taken = rest[:count]
+        del rest[:count]
+        return taken
+
+    axis_pairs = Axis(NP, pr, lambda j: (2 * j + c, z))
+    axis_z = Axis(S, z, lambda j: (d, j))
+    sums = []
+    for k, (base, count) in enumerate(split_rows(gA.shape[0], FF, 2 * FF, NP * S)):
+        axes = ([axis_x, axis_y] if k % 2 == 0 else [axis_y, axis_x]) + [axis_near, axis_far]
+        land = take(len(axes) + 1)
+        send, recv = take(2)
+        sums.append(Total(
+            remote, (sib, z), axes, own_cols, other_cols, gA, out_a, g_sem.at[k], base, count, land, send, recv,
+        ))
+    quarter = Dh // 2
+    side_cols = [pl.ds(pl.multiple_of(c * Dh + k * quarter, quarter), quarter) for k in range(2)]
+    for k in range(2):
+        land = take(2)
+        send, recv = take(2)
+        sums.append(Total(
+            remote, (sib, z), [axis_pairs, axis_z], side_cols[k], None, gB, out_b, g_sem.at[4 + k], 0, gB.shape[0],
+            land, send, recv,
+        ))
+    a1, a2, a3, a4, b1, b2 = sums
+
+    def advance(*several):
+        for each in several:
+            each.advance()
+
     up_row, down_row, out_row, gain_row = FF, 2 * FF, 3 * FF, 3 * FF + D
 
     loads = [
@@ -580,21 +595,28 @@
             target[base + first_row:base + last_row, :] = grad.astype(bf16)
 
     ff_grad(gA, 0, dga, nm)
-    sum_1.start(sum_1.core_scatter())
+    a1.begin()
     ff_grad(gA, up_row, dup, nm)
+    a2.begin()
     ff_grad(gA, down_row, hid, cots)
-    sum_2.start(sum_2.core_scatter())
+    a3.begin()
+    advance(a1)
     gA[out_row:out_row + D, :] = dot(mfull[...], da[...], 1, 0).astype(bf16)
     gA[gain_row:gain_row + 16, :] = jnp.concatenate([g_gm[...], jnp.zeros((8, D), f32)], axis=0).astype(bf16)
-    sum_3.start(sum_3.core_scatter())
-    sum_1.core_add()
+    a4.begin()
+    advance(a2, a3)
 
     dm_copy.wait()
     dOT[:, pl.ds(pl.multiple_of(c * half, half), half)] = dmT[own_rows, :]
-    sum_2.core_add()
-    sum_3.core_add()
-
     parts = (dga, dup, hid)
+
+    def lin_grads(side):
+        rows = slice(side * quarter, (side + 1) * quarter)
+        late = slice(Dh + side * quarter, Dh + (side + 1) * quarter)
+        for i in range(3):
+            grad = dot(parts[i][rows, 0:half], n_s[0:half, :], 1, 0)
+            grad = grad + dot(parts[i][late, 0:half], n_s[half:L, :], 1, 0)
+            gB[i * D:(i + 1) * D, side_cols[side]] = grad.T.astype(bf16)
 
     def unrotated(values, cosine, sine):
         a, b = values[:HD // 2], values[HD // 2:]
@@ -650,10 +672,21 @@
                 dacc_k[:, cols].astype(bf16).astype(f32), cos_s[:, cols], sin_s[:, cols]
             ).astype(bf16)
             parts[2][place_rows, 0:half] = dacc_v[:, cols].astype(bf16)
-        pl.when(h == 1)(sum_1.pair_add)
-
-    sum_2.pair_add()
-    sum_1.z_add()
+        @pl.when(h == 0)
+        def _():
+            advance(a4)
+
+        @pl.when(h == 1)
+        def _():
+            advance(a1, a2)
+            lin_grads(0)
+            b1.begin()
+
+        @pl.when(h == 2)
+        def _():
+            advance(a4, a3, a1, a2)
+
+    advance(a1, b1)
 
     def back_norm(side, start):
         side_rows = pl.ds(pl.multiple_of(side * Dh, Dh), Dh)
@@ -671,11 +704,9 @@
     dn_in = cots
     dn_copy = remote(nm, dn_in, dn_send.at[0], dn_recv.at[0], sib, z)
     dn_copy.start()
-
-    for i in range(3):
-        grad = dot(parts[i][0:Dh, 0:half], n_s[0:half, :], 1, 0)
-        grad = grad + dot(parts[i][Dh:2 * Dh, 0:half], n_s[half:L, :], 1, 0)
-        gB[i * D:(i + 1) * D, own_cols] = grad.T.astype(bf16)
+    advance(a2, a4, a3)
+    lin_grads(1)
+    advance(a1)
     back_wait(xs, (1 - c) * half, out, out_send, out_recv, loc_sem.at[pl.ds(2, per)])
     dn_copy.wait()
 
@@ -692,28 +723,27 @@
         g_ga[...] += fold_rows(d_normed * plain)
         d_start = inverse * (scaled - plain * jnp.mean(scaled * plain, axis=-1, keepdims=True))
         nm[rows, :] = (da[rows, :].astype(f32) + d_start).astype(bf16)
-        back_start(i, nm, start, gin, gin_send, gin_recv, loc_sem.at[pl.ds(2 + per, per)])
-
-    gB[3 * D:3 * D + 16, own_cols] = jnp.concatenate([g_ga[:, :Dh], g_ga[:, Dh:]], axis=0).astype(bf16)
-    sum_4.start(sum_4.pair_scatter())
-    sum_1.z_done()
-    sum_3.pair_add()
-    sum_2.z_add()
-    sum_1.pair_done()
-    sum_2.z_done()
-    sum_3.z_add()
-    sum_4.pair_add()
-    sum_3.z_done()
-    sum_1.core_done()
-    sum_2.pair_done()
-    sum_4.z_add()
-    sum_3.pair_done()
-    sum_4.z_done()
-    sum_2.core_done()
-    sum_4.pair_done()
-    sum_3.core_done()
+
+        @pl.when(i == 1)
+        def _():
+            advance(b1, a4)
+
+        @pl.when(i == 2)
+        def _():
+            advance(a2, a3)
+
+    advance(a1)
+    for k in range(D // quarter):
+        features = slice(k * quarter, (k + 1) * quarter)
+        gB[3 * D + 8 * k:3 * D + 8 * (k + 1), side_cols[1]] = g_ga[:, features].astype(bf16)
+    b2.begin()
+    for step in SCHEDULE:
+        if step < 6:
+            sums[step].advance()
+        else:
+            i = jnp.int32(step - 6)
+            back_start(i, nm, i * MB, gin, gin_send, gin_recv, loc_sem.at[pl.ds(2 + per, per)])
     back_wait(nm, 0, gin, gin_send, gin_recv, loc_sem.at[pl.ds(2 + per, per)])
-    sum_4.core_done()
 
 
 def on_device(
@@ -734,13 +764,15 @@
 
     strips = strip_offset(L // QB)
     shards = NP * S
-    RA, RB = padded(3 * FF + D + 16, shards), padded(3 * D + 16, shards)
-
-    def lands(rows, core):
-        kept = [buf(rows, Dh)] if core else []
-        return kept + [buf(NP - 1, rows // NP, Dh), buf(S - 1, rows // shards, Dh)]
-
-    steps = 2 + 2 * (NP - 1) + 2 * (S - 1)
+    RA, RB = padded(3 * FF + D + 16, shards), padded(3 * D + 32, shards)
+
+    sizes = axis_sizes(NP, S)
+    scattered = [(count, sizes[k % 2], True, Dh) for k, (_, count) in enumerate(split_rows(RA, FF, 2 * FF, shards))]
+    scattered += [(RB, sizes[2], False, Dh // 2)] * 2
+    sum_scratch = []
+    for count, over, core, width in scattered:
+        sum_scratch += [buf(*shape) for shape in lands(count, over, core, width)]
+        sum_scratch += [dma((copies_of(over),)), dma((copies_of(over),))]
     NB, per = half // MB, T // MB
     out, gin, out_a, out_b = pl.pallas_call(
         functools.partial(block_kernel, G, S, NP, T, L, D, FF),
@@ -762,11 +794,10 @@
             buf(half, D), buf(D, half),
             buf(Dh, L), buf(HD, L, dtype=f32), buf(HD, L, dtype=f32),
             buf(8, D, dtype=f32), buf(8, D, dtype=f32),
-            *(land for rows in split_rows(RA, FF, shards) for land in lands(rows, True)), *lands(RB, False),
             dma((7,)), dma((2 + 2 * per,)), dma((2,)), dma((G,)), dma((S,)), dma((S,)), dma((G,)), dma((G,)),
             dma((NH,)), dma((NH,)), dma((NB,)), dma((G * per,)), dma((1,)), dma((1,)), dma((1,)), dma((1,)),
-            dma((NB,)), dma((G * per,)), dma((4,)),
-            *([dma((steps,))] * 8),
+            dma((NB,)), dma((G * per,)), dma((6,)),
+            *sum_scratch,
         ],
         compiler_params=pltpu.CompilerParams(
             collective_id=0, has_side_effects=True, vmem_limit_bytes=63 * 2**20
@@ -776,14 +807,62 @@
         w_query, w_key, w_value, w_out, w_gate.T, w_up.T, w_down,
     )
 
-    last_a, last_b = 3 * FF + D, 3 * D
-    gain_attn = jnp.sum(out_b[last_b:last_b + 16].astype(f32).reshape(2, 8, 2, Dh), axis=(1, 2)).reshape(D)
-    gain_mlp = jnp.sum(out_a[last_a:last_a + 8].astype(f32), axis=0)
+    moves = []
+    for k in range(3):
+        moves += [(1, k * FF + first, FF // 2, k, first) for first in (0, FF // 2)]
+    moves.append((1, 3 * FF, D, 3, 0))
+    moves += [(2, k * D, D, 4 + k, 0) for k in range(3)]
+    moves += [(3, l * T, T, 7, l * T) for l in range(G)]
+
+    def convert_kernel(out_ref, a_ref, b_ref, gin_ref, *rest):
+        targets = rest[:8]
+        final_out, gain_a_out, gain_m_out = rest[8:11]
+        scratch = rest[11:]
+        lows, wides = scratch[:len(moves)], scratch[len(moves):2 * len(moves)]
+        tail_a, tail_b, out_low, read, write = scratch[2 * len(moves):]
+        sources = (out_ref, a_ref, b_ref, gin_ref)
+        last = len(moves)
+        extra = [
+            pltpu.make_async_copy(a_ref.at[pl.ds(3 * FF + D, 16)], tail_a, read.at[last]),
+            pltpu.make_async_copy(b_ref.at[pl.ds(3 * D, 32)], tail_b, read.at[last + 1]),
+            pltpu.make_async_copy(out_ref, out_low, read.at[last + 2]),
+        ]
+        reads, writes = [], []
+        for k, (source, row, rows, target, to) in enumerate(moves):
+            reads.append(pltpu.make_async_copy(sources[source].at[pl.ds(row, rows)], lows[k], read.at[k]))
+            writes.append(pltpu.make_async_copy(wides[k], targets[target].at[pl.ds(to, rows)], write.at[k]))
+        for copy in reads + extra:
+            copy.start()
+        for k in range(len(moves)):
+            reads[k].wait()
+            wides[k][...] = lows[k][...].astype(f32)
+            writes[k].start()
+        for copy in extra:
+            copy.wait()
+        final = pltpu.make_async_copy(out_low, final_out, write.at[last])
+        final.start()
+        gain_m_out[...] = jnp.sum(tail_a[0:8, :].astype(f32), axis=0)
+        tail = tail_b[:, Dh // 2:Dh].astype(f32) + tail_b[:, Dh + Dh // 2:].astype(f32)
+        gains = [jnp.sum(tail[8 * k:8 * (k + 1)], axis=0, keepdims=True) for k in range(4)]
+        gain_a_out[...] = jnp.concatenate(gains, axis=1).reshape(D)
+        for copy in writes + [final]:
+            copy.wait()
+
+    full = [(FF, D)] * 3 + [(D, D)] * 4 + [(G * T, D)]
+    results = pl.pallas_call(
+        convert_kernel,
+        out_shape=[jax.ShapeDtypeStruct(shape, f32) for shape in full]
+        + [jax.ShapeDtypeStruct((G * T, D), bf16), jax.ShapeDtypeStruct((D,), f32), jax.ShapeDtypeStruct((D,), f32)],
+        in_specs=[anywhere] * 4,
+        out_specs=[anywhere] * 9 + [vmem, vmem],
+        scratch_shapes=[buf(move[2], D) for move in moves] + [buf(move[2], D, dtype=f32) for move in moves]
+        + [buf(16, D), buf(32, D), buf(G * T, D), dma((len(moves) + 3,)), dma((len(moves) + 1,))],
+        compiler_params=pltpu.CompilerParams(vmem_limit_bytes=62 * 2**20),
+    )(out.reshape(G * T, D), out_a, out_b, gin.reshape(G * T, D))
+    g_gate, g_up, g_down, g_out, g_query, g_key, g_value, grad_input, output, gain_attn, gain_mlp = results
     return (
-        out, gin.astype(f32), gain_attn, gain_mlp,
-        out_b[:D].astype(f32), out_b[D:2 * D].astype(f32), out_b[2 * D:3 * D].astype(f32),
-        out_a[3 * FF:last_a].astype(f32), out_a[:FF].astype(f32).T, out_a[FF:2 * FF].astype(f32).T,
-        out_a[2 * FF:3 * FF].astype(f32),
+        output.reshape(G, T, D), grad_input.reshape(G, T, D), gain_attn, gain_mlp,
+        g_query, g_key, g_value, g_out, g_gate.T, g_up.T, g_down,
     )
 
 

time: 193 us -> 164 us (0.85)
  Pallas kernels: 177 us -> 163 us
  other arithmetic: 11.5 us -> 0 us
  local copies, waits for them, and re-layouts: 2.28 us -> 0 us
    pallas_call x1, Pallas kernels: 177 us -> 155 us  [on_device(): pl.pallas_call(functools.partial(block_kernel, G, S, NP, T, L, D, FF), ou...]
    convert_element_type x3 -> x0, other arithmetic: 10.1 us -> none  [the longest x1 3.81 us: on_device(): out_a[2 * FF:3 * FF].astype(f32)]
    pallas_call x0 -> x1, Pallas kernels: none -> 8.49 us  [on_device(): pl.pallas_call(convert_kernel, out_shape=[jax.ShapeDtypeStruct(shape, f32...]
where the time goes in v3:
time: 164 us
  Pallas kernels  163 us (99%)
    pallas_call x1, Pallas kernels, on_device(): pl.pallas_call(functools.partial(block_kernel, G, S, NP, T, L, D, FF), ou...  155 us
    pallas_call x1, Pallas kernels, on_device(): pl.pallas_call(convert_kernel, out_shape=[jax.ShapeDtypeStruct(shape, f32...  8.49 us

profile of v3, /device:TPU:0, one launch (start us, length us, event | category | flops | bytes accessed | tf_op | source)
XLA Modules:
  0.0 164.0 jit_solution(11350383724365829145)
XLA Ops:
  0.6 154.7 %shard_map.203 = (bf16[2,512,512]{2,1,0:T(8,128)(2,1)}, bf16[2,512,512]{2,1,0:T(8,128)(2,1)}, bf16[4864,512]{1,0:T(8,128)(2,1)}, bf16[1792,512]{1,0:T(8,128)(2,1)}) custom-call(bf16[2,512,512]{2,1,0:T(8,128)(2,1)} %x.1, s32[2,2048]{1,0:T(2,128)} %seg.1, bf16[2,512,512]{2,1,0:T(8,128)(2,1)} %cot.1, f32[1,512]{1,0:T(1,128)} %bitcast.14, f32[1,512]{1,0:T(1,128)} %bitcast.15, ...), custom_call_target="tpu_custom_call" | custom-call | tf_op jit(solution)/shard_map/pallas_call | solution.py:777
  155.3 8.5 %shard_map.204 = (f32[1376,512]{1,0:T(8,128)}, f32[1376,512]{1,0:T(8,128)}, f32[1376,512]{1,0:T(8,128)}, f32[512,512]{1,0:T(8,128)}, f32[512,512]{1,0:T(8,128)},...) custom-call(bf16[1024,512]{1,0:T(8,128)(2,1)} %bitcast.12, ...), custom_call_target="tpu_custom_call" | custom-call | tf_op jit(solution)/shard_map/pallas_call | solution.py:852

commit v4 on v3

--- a/solution.py
+++ b/solution.py
@@ -17,10 +17,22 @@
 bf16 = jnp.bfloat16
 QB = 256
 MB = 256
-SCHEDULE = (
-    4, 3, 1, 0, 2, 5, 3, 1, 2, 4, 6, 3, 5, 4, 2, 0, 1, 7, 3, 2, 8, 5,
-    0, 9, 0, 1, 1, 2, 3, 2, 3, 5, 5,
-)
+AXES = ("xynf", "yxnf", "xynf", "yxnf", "pz", "pz")
+CUT = 1
+SCHEDULE = {
+    "down": (0,),
+    "grads": (1, 2),
+    "head 0": (3,),
+    "head 1": (0, 1),
+    "head 2": (3, 2, 0, 1),
+    "head 3": (0, 4),
+    "parts": (1, 3, 2),
+    "projections": (0,),
+    "gin 1": (4, 3),
+    "gin 2": (1, 2),
+    "gin 3": (0,),
+    "end": (4, 3, 1, 0, 2, 5, 3, 1, 2, 4, 3, 5, 4, 2, 0, 1, 6, 3, 2, 7, 5, 0, 8, 0, 1, 1, 9, 2, 3, 2, 3, 5, 5),
+}
 EDGE = 128
 
 
@@ -142,16 +154,16 @@
     return jnp.sum(values.reshape(rows // 8, 8, width), axis=0)
 
 
-def split_rows(rows, first, second, shards):
+def sum_rows(RA, RB, D, FF, shards):
     unit = 16 * shards
-    edges = [0, first // unit * unit, second // unit * unit]
-    edges += [(edges[2] + rows + unit) // 2 // unit * unit, rows]
-    return [(start, end - start) for start, end in zip(edges, edges[1:])]
+    edges = [0, FF // unit * unit, 2 * FF // unit * unit]
+    edges += [min((edges[2] + RA + CUT * unit) // 2 // unit, 3 * FF // unit) * unit, RA]
+    return [(start, end - start) for start, end in zip(edges, edges[1:])] + [(0, padded(3 * D, shards)), (0, RB)]
 
 
 def axis_sizes(NP, S):
     fast = 2 if NP % 2 == 0 else 1
-    return [fast, NP // fast, 2, S // 2], [NP // fast, fast, 2, S // 2], [NP, S]
+    return {"x": fast, "y": NP // fast, "n": 2, "f": S // 2, "p": NP, "z": S}
 
 
 def interleave(main, count_main, side, count_side):
@@ -204,10 +216,14 @@
     fast = 2 if NP % 2 == 0 else 1
     row_at, col_at = pr // fast, lax.rem(pr, fast)
     low, high = lax.rem(z, 2), z // 2
-    axis_x = Axis(fast, col_at, lambda j: (2 * (row_at * fast + j) + c, z))
-    axis_y = Axis(NP // fast, row_at, lambda j: (2 * (j * fast + col_at) + c, z))
-    axis_near = Axis(2, low, lambda j: (d, high * 2 + j))
-    axis_far = Axis(S // 2, high, lambda j: (d, j * 2 + low))
+    axes = {
+        "x": Axis(fast, col_at, lambda j: (2 * (row_at * fast + j) + c, z)),
+        "y": Axis(NP // fast, row_at, lambda j: (2 * (j * fast + col_at) + c, z)),
+        "n": Axis(2, low, lambda j: (d, high * 2 + j)),
+        "f": Axis(S // 2, high, lambda j: (d, j * 2 + low)),
+        "p": Axis(NP, pr, lambda j: (2 * j + c, z)),
+        "z": Axis(S, z, lambda j: (d, j)),
+    }
     rest = list(rest)
 
     def take(count):
@@ -215,30 +231,23 @@
         del rest[:count]
         return taken
 
-    axis_pairs = Axis(NP, pr, lambda j: (2 * j + c, z))
-    axis_z = Axis(S, z, lambda j: (d, j))
+    quarter = Dh // 2
+    side_cols = [pl.ds(pl.multiple_of(c * Dh + k * quarter, quarter), quarter) for k in range(2)]
     sums = []
-    for k, (base, count) in enumerate(split_rows(gA.shape[0], FF, 2 * FF, NP * S)):
-        axes = ([axis_x, axis_y] if k % 2 == 0 else [axis_y, axis_x]) + [axis_near, axis_far]
-        land = take(len(axes) + 1)
+    for k, (base, count) in enumerate(sum_rows(gA.shape[0], gB.shape[0], D, FF, NP * S)):
+        core = k < 4
+        over = [axes[letter] for letter in AXES[k]]
+        land = take(len(over) + core)
         send, recv = take(2)
         sums.append(Total(
-            remote, (sib, z), axes, own_cols, other_cols, gA, out_a, g_sem.at[k], base, count, land, send, recv,
-        ))
-    quarter = Dh // 2
-    side_cols = [pl.ds(pl.multiple_of(c * Dh + k * quarter, quarter), quarter) for k in range(2)]
-    for k in range(2):
-        land = take(2)
-        send, recv = take(2)
-        sums.append(Total(
-            remote, (sib, z), [axis_pairs, axis_z], side_cols[k], None, gB, out_b, g_sem.at[4 + k], 0, gB.shape[0],
-            land, send, recv,
+            remote, (sib, z), over, own_cols if core else side_cols[k - 4], other_cols, gA if core else gB,
+            out_a if core else out_b, g_sem.at[k], base, count, land, send, recv,
         ))
     a1, a2, a3, a4, b1, b2 = sums
 
-    def advance(*several):
-        for each in several:
-            each.advance()
+    def step_at(place):
+        for each in SCHEDULE[place]:
+            sums[each].advance()
 
     up_row, down_row, out_row, gain_row = FF, 2 * FF, 3 * FF, 3 * FF + D
 
@@ -339,8 +348,12 @@
         kT[:, rows] = jnp.concatenate(rotated(Dh), axis=0).astype(bf16)
         vT[:, rows] = lin[2 * Dh:].astype(bf16)
 
+    def with_flipped(value, step):
+        bits = [lax.rem(value // 2 ** k, 2) for k in range(S.bit_length() - 1)]
+        return sum(2 ** k * (1 - bit if step // 2 ** k % 2 else bit) for k, bit in enumerate(bits))
+
     for step in range(S):
-        source = lax.rem(z + step, S)
+        source = with_flipped(z, step)
         arrived = remote(x.at[0], x_rows(source), x_send.at[0], x_recv.at[source], sib, z)
         if step == 0:
             @pl.when(gz == c)
@@ -528,47 +541,59 @@
     def _(i):
         start = pl.multiple_of(i * MB, MB)
         rows = pl.ds(start, MB)
-        mine = stays(i)
-
-        @pl.when((lax.rem(i, per) == 0) & jnp.logical_not(mine))
-        def _():
-            remote(cot.at[0], cot_rows(i // per), cot_send.at[0], cot_recv.at[i // per], sib, z).wait_recv()
-
-        @pl.when((lax.rem(i, per) == 0) & mine)
-        def _():
-            own_cot.wait()
-
         base = xs[pl.ds(pl.multiple_of(c * half + start, MB), MB), :].astype(f32)
         middle = base + dot(mfull[:, rows], wo_s[...], 0, 0)
-        plain, inverse = rms(middle)
-        gain = gain_m[...]
-        normed = (plain * gain).astype(bf16)
+        da[rows, :] = middle.astype(bf16)
+        plain, _ = rms(middle)
+        normed = (plain * gain_m[...]).astype(bf16)
         nm[rows, :] = normed
-        grad = cots[rows, :]
         result = middle
-        d_normed = None
         for first_col, last_col in ff_cuts:
             cut = slice(first_col, last_col)
             cut_up = slice(up_row + first_col, up_row + last_col)
             cut_down = slice(down_row + first_col, down_row + last_col)
             gate = dot(normed, gA[cut, :], 1, 1)
             up = dot(normed, gA[cut_up, :], 1, 1)
-            sig = 1.0 / (1.0 + jnp.exp(-gate))
-            act = gate * sig
-            hidden = (act * up).astype(bf16)
+            dga[rows, cut] = gate.astype(bf16)
+            dup[rows, cut] = up.astype(bf16)
+            hidden = (gate / (1.0 + jnp.exp(-gate)) * up).astype(bf16)
             hid[rows, cut] = hidden
             result = result + dot(hidden, gA[cut_down, :], 1, 0)
+        spare = pl.multiple_of((1 - c) * half + start, MB)
+        xs[pl.ds(spare, MB), :] = result.astype(bf16)
+        back_start(i, xs, spare, out, out_send, out_recv, loc_sem.at[pl.ds(2, per)])
+
+    @pl.loop(0, NB)
+    def _(i):
+        start = pl.multiple_of(i * MB, MB)
+        rows = pl.ds(start, MB)
+        mine = stays(i)
+
+        @pl.when((lax.rem(i, per) == 0) & jnp.logical_not(mine))
+        def _():
+            remote(cot.at[0], cot_rows(i // per), cot_send.at[0], cot_recv.at[i // per], sib, z).wait_recv()
+
+        @pl.when((lax.rem(i, per) == 0) & mine)
+        def _():
+            own_cot.wait()
+
+        plain, inverse = rms(da[rows, :].astype(f32))
+        grad = cots[rows, :]
+        d_normed = None
+        for first_col, last_col in ff_cuts:
+            cut = slice(first_col, last_col)
+            cut_up = slice(up_row + first_col, up_row + last_col)
+            cut_down = slice(down_row + first_col, down_row + last_col)
+            gate, up = dga[rows, cut].astype(f32), dup[rows, cut].astype(f32)
+            sig = 1.0 / (1.0 + jnp.exp(-gate))
             d_hidden = dot(grad, gA[cut_down, :], 1, 1)
             d_gate = (d_hidden * up * sig * (1.0 + gate * (1.0 - sig))).astype(bf16)
-            d_up = (d_hidden * act).astype(bf16)
+            d_up = (d_hidden * (gate * sig)).astype(bf16)
             dga[rows, cut] = d_gate
             dup[rows, cut] = d_up
             term = dot(d_gate, gA[cut, :], 1, 0) + dot(d_up, gA[cut_up, :], 1, 0)
             d_normed = term if d_normed is None else d_normed + term
-        spare = pl.multiple_of((1 - c) * half + start, MB)
-        xs[pl.ds(spare, MB), :] = result.astype(bf16)
-        back_start(i, xs, spare, out, out_send, out_recv, loc_sem.at[pl.ds(2, per)])
-        scaled = d_normed * gain
+        scaled = d_normed * gain_m[...]
         g_gm[...] += fold_rows(d_normed * plain)
         d_middle = grad.astype(f32) + inverse * (scaled - plain * jnp.mean(scaled * plain, axis=-1, keepdims=True))
         d_attn = d_middle.astype(bf16)
@@ -600,11 +625,11 @@
     a2.begin()
     ff_grad(gA, down_row, hid, cots)
     a3.begin()
-    advance(a1)
+    step_at("down")
     gA[out_row:out_row + D, :] = dot(mfull[...], da[...], 1, 0).astype(bf16)
     gA[gain_row:gain_row + 16, :] = jnp.concatenate([g_gm[...], jnp.zeros((8, D), f32)], axis=0).astype(bf16)
     a4.begin()
-    advance(a2, a3)
+    step_at("grads")
 
     dm_copy.wait()
     dOT[:, pl.ds(pl.multiple_of(c * half, half), half)] = dmT[own_rows, :]
@@ -674,19 +699,19 @@
             parts[2][place_rows, 0:half] = dacc_v[:, cols].astype(bf16)
         @pl.when(h == 0)
         def _():
-            advance(a4)
+            step_at("head 0")
 
         @pl.when(h == 1)
         def _():
-            advance(a1, a2)
+            step_at("head 1")
             lin_grads(0)
             b1.begin()
 
         @pl.when(h == 2)
         def _():
-            advance(a4, a3, a1, a2)
-
-    advance(a1, b1)
+            step_at("head 2")
+
+    step_at("head 3")
 
     def back_norm(side, start):
         side_rows = pl.ds(pl.multiple_of(side * Dh, Dh), Dh)
@@ -704,9 +729,9 @@
     dn_in = cots
     dn_copy = remote(nm, dn_in, dn_send.at[0], dn_recv.at[0], sib, z)
     dn_copy.start()
-    advance(a2, a4, a3)
+    step_at("parts")
     lin_grads(1)
-    advance(a1)
+    step_at("projections")
     back_wait(xs, (1 - c) * half, out, out_send, out_recv, loc_sem.at[pl.ds(2, per)])
     dn_copy.wait()
 
@@ -726,18 +751,18 @@
 
         @pl.when(i == 1)
         def _():
-            advance(b1, a4)
+            step_at("gin 1")
 
         @pl.when(i == 2)
         def _():
-            advance(a2, a3)
-
-    advance(a1)
+            step_at("gin 2")
+
+    step_at("gin 3")
     for k in range(D // quarter):
         features = slice(k * quarter, (k + 1) * quarter)
         gB[3 * D + 8 * k:3 * D + 8 * (k + 1), side_cols[1]] = g_ga[:, features].astype(bf16)
     b2.begin()
-    for step in SCHEDULE:
+    for step in SCHEDULE["end"]:
         if step < 6:
             sums[step].advance()
         else:
@@ -767,11 +792,10 @@
     RA, RB = padded(3 * FF + D + 16, shards), padded(3 * D + 32, shards)
 
     sizes = axis_sizes(NP, S)
-    scattered = [(count, sizes[k % 2], True, Dh) for k, (_, count) in enumerate(split_rows(RA, FF, 2 * FF, shards))]
-    scattered += [(RB, sizes[2], False, Dh // 2)] * 2
     sum_scratch = []
-    for count, over, core, width in scattered:
-        sum_scratch += [buf(*shape) for shape in lands(count, over, core, width)]
+    for k, (_, count) in enumerate(sum_rows(RA, RB, D, FF, shards)):
+        over = [sizes[letter] for letter in AXES[k]]
+        sum_scratch += [buf(*shape) for shape in lands(count, over, k < 4, Dh if k < 4 else Dh // 2)]
         sum_scratch += [dma((copies_of(over),)), dma((copies_of(over),))]
     NB, per = half // MB, T // MB
     out, gin, out_a, out_b = pl.pallas_call(

time: 164 us -> 161 us (0.982)
  Pallas kernels: 163 us -> 160 us
    pallas_call x1, Pallas kernels: 155 us -> 152 us  [on_device(): pl.pallas_call(functools.partial(block_kernel, G, S, NP, T, L, D, FF), ou...]
where the time goes in v4:
time: 161 us
  Pallas kernels  160 us (99%)
    pallas_call x1, Pallas kernels, on_device(): pl.pallas_call(functools.partial(block_kernel, G, S, NP, T, L, D, FF), ou...  152 us
    pallas_call x1, Pallas kernels, on_device(): pl.pallas_call(convert_kernel, out_shape=[jax.ShapeDtypeStruct(shape, f32...  8.49 us

profile of v4, /device:TPU:0, one launch (start us, length us, event | category | flops | bytes accessed | tf_op | source)
XLA Modules:
  0.0 160.9 jit_solution(10183674502994999763)
XLA Ops:
  0.6 151.6 %shard_map.203 = (bf16[2,512,512]{2,1,0:T(8,128)(2,1)}, bf16[2,512,512]{2,1,0:T(8,128)(2,1)}, bf16[4864,512]{1,0:T(8,128)(2,1)}, bf16[1792,512]{1,0:T(8,128)(2,1)}) custom-call(bf16[2,512,512]{2,1,0:T(8,128)(2,1)} %x.1, s32[2,2048]{1,0:T(2,128)} %seg.1, bf16[2,512,512]{2,1,0:T(8,128)(2,1)} %cot.1, f32[1,512]{1,0:T(1,128)} %bitcast.14, f32[1,512]{1,0:T(1,128)} %bitcast.15, ...), custom_call_target="tpu_custom_call" | custom-call | tf_op jit(solution)/shard_map/pallas_call | solution.py:801
  152.3 8.5 %shard_map.204 = (f32[1376,512]{1,0:T(8,128)}, f32[1376,512]{1,0:T(8,128)}, f32[1376,512]{1,0:T(8,128)}, f32[512,512]{1,0:T(8,128)}, f32[512,512]{1,0:T(8,128)},...) custom-call(bf16[1024,512]{1,0:T(8,128)(2,1)} %bitcast.12, ...), custom_call_target="tpu_custom_call" | custom-call | tf_op jit(solution)/shard_map/pallas_call | solution.py:876
